TPU v7x, 512 devices: a whole 4x4x16 slice. The times are simulated.
512 devices in a mesh: occ: 8 (over x_lo, y), vir: 64 (over z, x_hi, core).
Axes of the slice: x: 4 (x_hi: 2, x_lo: 2; x = x_hi * 2 + x_lo), y: 4, z: 16, core: 2. Of those that a mesh axis runs over, the one named last changes fastest.
Arguments:
- amplitudes: float32 [1600, 230400], P('occ', 'vir'), may hold values from -6 to 6
- singles: float32 [40, 480], replicated, may hold values from -3 to 3
- integrals: float32 [2, 230400, 256], P(None, 'vir', 'occ'), may hold values from -0.1875 to 0.1875
- occ_irrep: int32 [40], replicated, may hold values from 0 to 7, never falling along the last dimension, each value on 1 to 10 neighbouring positions
- vir_irrep: int32 [480], replicated, may hold values from 0 to 7, never falling along the last dimension, each value on 1 to 120 neighbouring positions
- owner: int32 [64], replicated, may hold values from 0 to 63, each once
Outputs:
- residual: float32 [1600, 512], P('occ', 'vir')
Inputs may be any that keep to these rules, and one draw needn't show every extreme that they name: `occ_irrep`: labels never fall from one orbital to the next; each of the 8 irreps holds between 1 and 10 orbitals, one exactly that many. `vir_irrep`: labels never fall from one orbital to the next; each of the 8 irreps holds between 1 and 120 orbitals, one exactly that many. `owner`: every vir index owns exactly one block.
All inputs are finite; a program needn't handle non-finite values.
Results may differ from a plain program's by a relative error of at most 0.0003.
Values sent between devices are 32-bit elements; how exact they have to be, the bound alone decides.
No kernel may reach another device: no remote copies, remote signals or barrier semaphores. Data moves between devices by JAX's collectives and lax.ppermute only.
A program may use at most 64 MiB of HBM per device.

v0:
```python
import jax
import jax.numpy as jnp
from jax import lax
from jax.sharding import PartitionSpec as P

SPAN = 256


highest = lax.Precision.HIGHEST


def pair_parts(first, count, width):
    index = first + jnp.arange(count, dtype=jnp.int32)
    return (index // width, index % width)


def pick_table(length, picks):
    return jnp.arange(length, dtype=jnp.int32)[:, None] == picks[None, :]


def lookup(table, picks):
    chosen = pick_table(table.shape[0], picks)
    return jnp.sum(jnp.where(chosen, table[:, None], 0), axis=0)


def arrange(part, keep, inverse, width):
    masked = jnp.where(keep, part, jnp.float32(0.0))
    grouped = masked.reshape(part.shape[0], inverse.shape[0], width)
    return jnp.take(grouped, inverse, axis=1)


def shards(amplitudes, singles, integrals, occ_irrep, vir_irrep, owner):
    pair_rows, pair_cols = amplitudes.shape
    occ_count = occ_irrep.shape[0]
    vir_count = vir_irrep.shape[0]
    occ_rows = pair_rows // occ_count
    occ_first = lax.axis_index("occ") * occ_rows
    cd_first = lax.axis_index("vir") * pair_cols
    first_orbital, second_orbital = pair_parts(cd_first, pair_cols, vir_count)
    singles_sym = jnp.where(occ_irrep[:, None] == vir_irrep[None, :], singles, jnp.float32(0.0))
    rows_local = lax.dynamic_slice_in_dim(singles_sym, occ_first, occ_rows, 0)
    occ_local = lax.dynamic_slice_in_dim(occ_irrep, occ_first, occ_rows, 0)
    pick_first = pick_table(vir_count, first_orbital).astype(jnp.float32)
    pick_second = pick_table(vir_count, second_orbital).astype(jnp.float32)
    left_terms = jnp.dot(rows_local, pick_first, precision=highest)
    right_terms = jnp.dot(singles_sym, pick_second, precision=highest)
    sym_cd = jnp.bitwise_xor(lookup(vir_irrep, first_orbital), lookup(vir_irrep, second_orbital))
    sym_ij = jnp.bitwise_xor(occ_local[:, None], occ_irrep[None, :])
    blocks = amplitudes.reshape(occ_rows, occ_count, pair_cols)
    tau_rows = jnp.where(
        sym_ij[:, :, None] == sym_cd[None, None, :],
        blocks + left_terms[:, None, :] * right_terms[None, :, :],
        jnp.float32(0.0),
    )
    tau_rows = tau_rows.reshape(pair_rows, pair_cols)
    sym_rows = sym_ij.reshape(pair_rows)
    block_count = owner.shape[0]
    block_ids = jnp.arange(block_count, dtype=jnp.int32)
    matches = owner[:, None] == block_ids[None, :]
    inverse = jnp.sum(jnp.where(matches, block_ids[:, None], 0), axis=0)
    width = SPAN // block_count
    results = []
    for span_index in range(2):
        part = 0.5 * jnp.dot(
            tau_rows,
            lax.all_gather(integrals[span_index], "occ", axis=1, tiled=True),
            precision=highest,
        )
        first_ab, second_ab = pair_parts(span_index * SPAN, SPAN, vir_count)
        sym_ab = jnp.bitwise_xor(lookup(vir_irrep, first_ab), lookup(vir_irrep, second_ab))
        ordered = arrange(part, sym_rows[:, None] == sym_ab[None, :], inverse, width).reshape(
            pair_rows, SPAN
        )
        results.append(lax.psum_scatter(ordered, "vir", scatter_dimension=1, tiled=True))
    return jnp.concatenate(results, axis=1)


def solution(mesh):
    placed = (P("occ", "vir"), P(), P(None, "vir", "occ"), P(), P(), P())
    return jax.shard_map(
        shards, mesh=mesh, in_specs=placed, out_specs=P("occ", "vir"), check_vma=False
    )
```

profile of v0, /device:TPU:1, one launch (start us, length us, event | category | flops | bytes accessed | tf_op | source)
XLA Modules:
  0.0 671.3 jit_solution(1337013209753657724)
XLA Ops:
  6.5 0.0 copy-start.3
  6.5 0.0 copy-start.2
  6.5 0.0 copy-start.4
  6.5 0.0 all-gather.5.cloned.1.call-start
  6.6 2.2 fusion.32
  8.8 0.0 all-gather.5.cloned.1.call-update
  8.8 0.0 all-gather.7.cloned.1.call-start
  8.9 0.7 all-gather.7.cloned.1.call-update
  9.6 0.0 all-reduce.5.cloned.1.call-start
  9.7 0.7 dynamic_slice.6
  10.4 0.1 xor.52
  10.5 0.1 xor.53
  10.5 0.7 xor.54
  11.2 0.1 xor.55
  11.3 0.7 broadcast_reduce_fusion
  11.9 0.1 xor.59
  12.1 2.8 select_reduce_fusion
  14.9 0.0 copy-done.2
  15.0 0.3 select_reduce_fusion.4
  15.3 0.0 copy-done.4
  15.3 0.1 select_reduce_fusion.6
  15.4 0.0 copy-done.3
  15.4 0.0 copy-done.1
  15.4 0.1 compare_select_fusion
  15.5 2.3 fusion.1
  17.9 2.6 fusion
  20.4 0.2 broadcast_multiply_fusion
  20.6 0.0 copy-done
  20.7 0.5 fusion.8
  21.2 50.2 %all-gather.5.cloned.1.call-done = f32[1,3600,256]{1,2,0:T(8,128)} async-done(((f32[1,3600,32]{1,2,0:T(8,128)}), f32[1,3600,256]{1,2,0:T(8,128)}) %all-gather.5.cloned.1.call-update) | async-done | bytes 3686416 | tf_op jit(solution)/shard_map/all_gather | solution.py:66
  71.4 5.3 fusion.18
  76.7 0.1 copy.13
  76.8 0.1 reshape.128
  76.9 52.4 %all-gather.7.cloned.1.call-done = f32[1,3600,256]{1,2,0:T(8,128)} async-done(((f32[1,3600,32]{1,2,0:T(8,128)}), f32[1,3600,256]{1,2,0:T(8,128)}) %all-gather.7.cloned.1.call-update) | async-done | bytes 3686416 | tf_op jit(solution)/shard_map/all_gather | solution.py:66
  129.3 5.5 fusion.15
  134.8 0.1 copy.14
  134.9 0.1 reshape.130
  135.0 0.7 gather_fusion
  135.7 0.7 gather_fusion.1
  136.4 0.2 select_bitcast_fusion.1
  136.6 0.8 reshape.131
  137.4 0.8 reshape.129
  138.2 0.0 all-reduce.5.cloned.1.call-update
  138.3 1.3 dynamic-slice
  140.2 522.6 %all-reduce.5.cloned.1.call-done = (f32[200,256]{0,1:T(8,128)}, f32[200,256]{0,1:T(8,128)}) async-done(((f32[200,256]{0,1:T(8,128)}, f32[200,256]{0,1:T(8,128)}), (f32[200,256]{0,1:T(8,128)}, f32[200,256]{0,1:T(8,128)})) %all-reduce.5.cloned.1.call-update) | async-done | bytes 409616
  662.8 0.7 constant_dynamic-slice_fusion
  663.5 0.7 constant_dynamic-slice_fusion.1
  664.2 0.6 pad_maximum_fusion
  (12 shorter events, 0.1 us)
Async XLA Ops:
  6.5 8.9 %copy-start.3 = (s32[40]{0:T(128)S(1)}, s32[40]{0:T(128)}, u32[]{:S(2)}) copy-start(s32[40]{0:T(128)} %param.11) | copy-start | bytes 484
  6.5 8.4 %copy-start.2 = (s32[480]{0:T(512)S(1)}, s32[480]{0:T(512)}, u32[]{:S(2)}) copy-start(s32[480]{0:T(512)} %param.12) | copy-start | bytes 5764
  6.5 8.7 %copy-start.4 = (s32[64]{0:T(128)S(1)}, s32[64]{0:T(128)}, u32[]{:S(2)}) copy-start(s32[64]{0:T(128)} %param.13) | copy-start | bytes 772
  6.5 8.9 %copy-start.1 = (f32[40,480]{1,0:T(8,128)S(1)}, f32[40,480]{1,0:T(8,128)}, u32[]{:S(2)}) copy-start(f32[40,480]{1,0:T(8,128)} %param.9) | copy-start | bytes 230404
  6.5 64.8 %all-gather.5.cloned.1.call-start = ((), (), s32[]{:S(2)}) async-start(), calls=%async_computation | async-start | bytes 4276224 | tf_op jit(solution)/shard_map/all_gather | solution.py:66
  8.8 120.4 %all-gather.7.cloned.1.call-start = ((), (), s32[]{:S(2)}) async-start(), calls=%async_computation.1 | async-start | bytes 4276224 | tf_op jit(solution)/shard_map/all_gather | solution.py:66
  9.6 653.2 %all-reduce.5.cloned.1.call-start = ((), (), s32[]{:S(2)}) async-start(), calls=%async_computation.2 | async-start | bytes 1048576
  17.9 2.8 copy-start
Sparse Core Ops, SparseCore 0:
  9.5 61.8 all-gather.4
  73.5 55.7 all-gather.6
  138.4 524.3 all-reduce.4
where the time goes:
time: 672 us; the launch traced here: 671 us
  waiting for transfers between devices  626 us (93%)
  matrix products  15.7 us (2%)
  between operations  14 us (2%)
  local copies, waits for them, and re-layouts  10.7 us (2%)
    unnamed x4, waiting for transfers between devices  523 us
    all_gather x2, waiting for transfers between devices, shards(): lax.all_gather(integrals[span_index], 'occ', axis=1, tiled=True)  103 us
  transfers between devices with their start and end apart: 3, of which 3 were waited for; matrix products, arithmetic and copies ran while one was open for 3% of the time, Pallas kernels for 0%

commit v1 on v0

v1 whole, which is shorter than its diff:
```python
import functools

import jax
import jax.numpy as jnp
from jax import lax
from jax.experimental import pallas as pl
from jax.experimental.pallas import tpu as pltpu
from jax.sharding import PartitionSpec as P

NO = 40
NV = 480
SPAN = 256
IRREPS = 8
RUN_V = 120
RUN_O = 10
ROWS_I = 5
COLS = 32
CD = 3600
SLOTS = 8
LEAD = 256
WIDE = 33 * 128
MAIN = 28 * 128
GROUP = 64
PACK = 2 * SLOTS * RUN_V
VMEM = 32 * 1024 * 1024


def placed():
    return lax.axis_index("occ"), lax.axis_index("vir")


def fill_starts(labels, length, starts):
    top = 1
    while top * 2 <= length:
        top *= 2
    starts[0] = jnp.int32(0)
    starts[IRREPS] = jnp.int32(length)
    for g in range(1, IRREPS):
        low = jnp.int32(0)
        bit = top
        while bit:
            cand = low + bit
            below = labels[jnp.minimum(cand, length) - 1] < g
            low = jnp.where((cand <= length) & below, cand, low)
            bit //= 2
        starts[g] = low


def irrep_of(index, starts):
    total = jnp.zeros_like(index)
    for g in range(1, IRREPS):
        total += (index >= starts[g]).astype(jnp.int32)
    return total


def join(near, far, position):
    shift = lax.rem(position, 128)
    back = lax.rem(128 - shift, 128)
    lanes = lax.broadcasted_iota(jnp.int32, near.shape, 1)
    return jnp.where(
        lanes < 128 - shift, pltpu.roll(near, back, axis=1), pltpu.roll(far, back, axis=1)
    )


def window(ref, lead, position):
    base = pl.multiple_of((position // 128) * 128, 128)
    near = ref[lead + (pl.ds(base, 128),)]
    far = ref[lead + (pl.ds(base + 128, 128),)]
    return join(near, far, position)


def tile_window(ref, rows, position):
    tile = position // 128
    return join(ref[tile, rows, :], ref[tile + 1, rows, :], position)


def place_slot(ref, rows, slot, value, lanes):
    tile, inner = divmod(slot * RUN_V, 128)
    if inner == 0:
        ref[rows, pl.ds(tile * 128, 128)] = value
        return
    turned = pltpu.roll(value, inner, axis=1)
    old = ref[rows, pl.ds(tile * 128, 128)]
    ref[rows, pl.ds(tile * 128, 128)] = jnp.where(lanes >= inner, turned, old)
    if slot == SLOTS - 1:
        turned = jnp.where(lanes < SLOTS * RUN_V - (tile + 1) * 128, turned, 0.0)
    ref[rows, pl.ds((tile + 1) * 128, 128)] = turned


def pack_kernel(
    where_am_i,
    vir_ref,
    occ_ref,
    amp_hbm,
    amp_tail,
    int_hbm,
    int_tail,
    singles_ref,
    packed_ref,
    high_ref,
    low_ref,
    vstart,
    ostart,
    ints,
    amps,
    chunk,
    group,
    ones,
    single_win,
    left,
    sems,
):
    int_copy = pltpu.make_async_copy(
        int_hbm.at[:, :, pl.ds(0, MAIN)], ints.at[:, :, pl.ds(LEAD, MAIN)], sems.at[0]
    )
    amp_copies = [
        pltpu.make_async_copy(
            amp_hbm.at[:, pl.ds(t * 128, 128)],
            amps.at[LEAD // 128 + t, pl.ds(0, ROWS_I * NO), :],
            sems.at[1 + t],
        )
        for t in range(MAIN // 128)
    ]
    int_copy.start()
    for copy in amp_copies:
        copy.start()
    o, v = where_am_i()
    fill_starts(vir_ref, NV, vstart)
    fill_starts(occ_ref, NO, ostart)
    c_first = (v * 15) // 2
    offset = (v % 2) * (NV // 2)

    tail = CD - MAIN
    ints[:, :, pl.ds(0, LEAD)] = jnp.zeros((2, COLS, LEAD), jnp.float32)
    lanes3 = lax.broadcasted_iota(jnp.int32, (2, COLS, 128), 2)
    ints[:, :, pl.ds(LEAD + MAIN, 128)] = jnp.where(lanes3 < tail, int_tail[...], 0.0)
    rest = WIDE - LEAD - MAIN - 128
    ints[:, :, pl.ds(LEAD + MAIN + 128, rest)] = jnp.zeros((2, COLS, rest), jnp.float32)
    amps[(LEAD + MAIN) // 128, pl.ds(0, ROWS_I * NO), :] = amp_tail[...]
    amps[:, pl.ds(ROWS_I * NO, 16), :] = jnp.zeros((WIDE // 128, 16, 128), jnp.float32)

    int_copy.wait()
    lanes = lax.broadcasted_iota(jnp.int32, (COLS, 128), 1)
    row = lax.broadcasted_iota(jnp.int32, (COLS, 128), 0)
    for s in range(2):
        first = s * SPAN + o * COLS
        a = (first >= NV).astype(jnp.int32)
        b = first - a * NV
        irr_a = vir_ref[a]
        irr_b = irrep_of(row + b, vstart)
        low_h = vir_ref[b]
        high_h = vir_ref[b + COLS - 1]
        for slot in range(SLOTS):
            irr_c = vir_ref[c_first + slot]
            turn = irr_c ^ irr_a

            def one(h, value, slot=slot, turn=turn, irr_b=irr_b, s=s):
                position = LEAD + slot * NV + vstart[turn ^ h] - offset
                return jnp.where(irr_b == h, window(ints, (s, slice(None)), position), value)

            value = lax.fori_loop(low_h, high_h + 1, one, jnp.zeros((COLS, 128), jnp.float32))
            place_slot(chunk.at[s], pl.ds(0, COLS), slot, value, lanes)
    full = 7 * 128
    packed_ref[:, pl.ds(0, full)] = chunk[0, :, pl.ds(0, full)]
    packed_ref[:, pl.ds(full, 128)] = jnp.where(
        lanes < 64,
        chunk[0, :, pl.ds(full, 128)],
        pltpu.roll(chunk[1, :, pl.ds(full, 128)], 64, axis=1),
    )
    packed_ref[:, pl.ds(full + 128, full)] = chunk[1, :, pl.ds(0, full)]

    ones[...] = jnp.zeros_like(ones)
    for t in range(4):
        size = min(128, NV - t * 128)
        ones[t, pl.ds(0, NO), pl.ds(0, size)] = singles_ref[:, pl.ds(t * 128, size)]
    for g in range(IRREPS):
        single_win[g] = tile_window(ones, pl.ds(ostart[g], 16), vstart[g])
    lane_c = lax.broadcasted_iota(jnp.int32, (8, 128), 1)
    row_i = lax.broadcasted_iota(jnp.int32, (8, 1), 0)
    irr_i = [occ_ref[o * ROWS_I + i] for i in range(ROWS_I)]
    for slot in range(SLOTS):
        c = c_first + slot
        irr_c = vir_ref[c]
        own = ones[c // 128, pl.ds(o * ROWS_I, 8), :]
        column = jnp.sum(jnp.where(lane_c == lax.rem(c, 128), own, 0.0), axis=1, keepdims=True)
        for i in range(ROWS_I):
            column = jnp.where((row_i == i) & (irr_i[i] != irr_c), 0.0, column)
        left[slot] = jnp.broadcast_to(column, (8, 128))

    for copy in amp_copies:
        copy.wait()
    lanes_o = lax.broadcasted_iota(jnp.int32, (RUN_O, 128), 1)
    group[...] = jnp.zeros_like(group)

    def symmetry(sym, carry):
        for slot in range(SLOTS):
            g = vir_ref[c_first + slot] ^ sym
            begin = slot * NV + vstart[g] - offset
            from_lane = jnp.maximum(0, -begin)
            to_lane = jnp.minimum(vstart[g + 1] - vstart[g], CD - begin)
            keep = (lanes_o >= from_lane) & (lanes_o < to_lane)
            for i in range(ROWS_I):
                j_rows = pl.ds(i * NO + ostart[irr_i[i] ^ sym], RUN_O)
                value = tile_window(amps, j_rows, LEAD + begin)
                product = left[slot, pl.ds(i, 1), :] * single_win[g, pl.ds(0, RUN_O), :]
                value = jnp.where(keep, value + product, 0.0)
                place_slot(group, pl.ds(i * RUN_O, RUN_O), slot, value, lanes_o)
        whole = group[...]
        top = whole.astype(jnp.bfloat16)
        out = pl.ds(pl.multiple_of(sym * GROUP, GROUP), GROUP)
        high_ref[out, :] = top
        low_ref[out, :] = (whole - top.astype(jnp.float32)).astype(jnp.bfloat16)
        return carry

    lax.fori_loop(0, IRREPS, symmetry, 0)


def pack(where_am_i, amplitudes, singles, integrals_t, occ_irrep, vir_irrep):
    depth = SLOTS * 128
    smem = pl.BlockSpec(memory_space=pltpu.SMEM)
    vmem = pl.BlockSpec(memory_space=pltpu.VMEM)
    return pl.pallas_call(
        functools.partial(pack_kernel, where_am_i),
        grid=(1,),
        in_specs=[
            smem,
            smem,
            pl.BlockSpec(memory_space=pl.ANY),
            pl.BlockSpec((ROWS_I * NO, 128), lambda n: (0, MAIN // 128)),
            pl.BlockSpec(memory_space=pl.ANY),
            pl.BlockSpec((2, COLS, 128), lambda n: (0, 0, MAIN // 128)),
            vmem,
        ],
        out_specs=[vmem, vmem, vmem],
        out_shape=[
            jax.ShapeDtypeStruct((COLS, PACK), jnp.float32),
            jax.ShapeDtypeStruct((IRREPS * GROUP, depth), jnp.bfloat16),
            jax.ShapeDtypeStruct((IRREPS * GROUP, depth), jnp.bfloat16),
        ],
        scratch_shapes=[
            pltpu.SMEM((IRREPS + 1,), jnp.int32),
            pltpu.SMEM((IRREPS + 1,), jnp.int32),
            pltpu.VMEM((2, COLS, WIDE), jnp.float32),
            pltpu.VMEM((WIDE // 128, ROWS_I * NO + 16, 128), jnp.float32),
            pltpu.VMEM((2, COLS, depth), jnp.float32),
            pltpu.VMEM((GROUP, depth), jnp.float32),
            pltpu.VMEM((5, NO + 16, 128), jnp.float32),
            pltpu.VMEM((IRREPS, 16, 128), jnp.float32),
            pltpu.VMEM((SLOTS, 8, 128), jnp.float32),
            pltpu.SemaphoreType.DMA((1 + MAIN // 128,)),
        ],
        compiler_params=pltpu.CompilerParams(vmem_limit_bytes=VMEM),
        name="pack",
    )(vir_irrep, occ_irrep, amplitudes, amplitudes, integrals_t, integrals_t, singles)


def ladder_kernel(vir_ref, owner_ref, packed_ref, high_ref, low_ref, out_ref, vstart, top, bottom):
    fill_starts(vir_ref, NV, vstart)
    full = 7 * 128
    for source in range(8):
        for s in range(2):
            wide = packed_ref[source, :, pl.ds(s * (full + 128), full)]
            last = packed_ref[source, :, pl.ds(full, 128)]
            if s == 1:
                last = pltpu.roll(last, 64, axis=1)
            rows = pl.ds(s * SPAN + source * COLS, COLS)
            for part, at, size in ((wide, 0, full), (last, full, 128)):
                upper = part.astype(jnp.bfloat16)
                top[rows, pl.ds(at, size)] = upper
                bottom[rows, pl.ds(at, size)] = (part - upper.astype(jnp.float32)).astype(jnp.bfloat16)
    contract = functools.partial(
        lax.dot_general,
        dimension_numbers=(((1,), (1,)), ((), ())),
        preferred_element_type=jnp.float32,
    )
    upper, lower = top[...], bottom[...]
    high, low = high_ref[...], low_ref[...]
    sums = contract(upper, high) + contract(lower, high) + contract(upper, low)
    column = lax.broadcasted_iota(jnp.int32, (2 * SPAN, 128), 0)
    second = column >= NV
    sym = irrep_of(jnp.where(second, column - NV, column), vstart)
    sym = sym ^ jnp.where(second, vir_ref[1], vir_ref[0])
    pair = sym >> 1
    picked = sums[:, 0:128]
    for t in range(1, 4):
        picked = jnp.where(pair == t, sums[:, t * 128 : (t + 1) * 128], picked)
    span = (column >= SPAN).astype(jnp.int32)
    picked = jnp.where((sym & 1) == span, picked, pltpu.roll(picked, 64, axis=1))
    lanes = lax.broadcasted_iota(jnp.int32, (SPAN, 128), 1)
    both = 0.5 * jnp.where(lanes < 64, picked[:SPAN], picked[SPAN:])
    for k in range(64):
        out_ref[owner_ref[k]] = both[4 * k : 4 * k + 4, :]


def ladder(packed, high, low, vir_irrep, owner):
    smem = pl.BlockSpec(memory_space=pltpu.SMEM)
    vmem = pl.BlockSpec(memory_space=pltpu.VMEM)
    return pl.pallas_call(
        ladder_kernel,
        in_specs=[smem, smem, vmem, vmem, vmem],
        out_specs=vmem,
        out_shape=jax.ShapeDtypeStruct((64, 4, 128), jnp.float32),
        scratch_shapes=[
            pltpu.SMEM((IRREPS + 1,), jnp.int32),
            pltpu.VMEM((2 * SPAN, SLOTS * 128), jnp.bfloat16),
            pltpu.VMEM((2 * SPAN, SLOTS * 128), jnp.bfloat16),
        ],
        compiler_params=pltpu.CompilerParams(vmem_limit_bytes=VMEM),
        name="ladder",
    )(vir_irrep, owner, packed, high, low)


def finish_kernel(where_am_i, vir_ref, occ_ref, owner_ref, parts_ref, out_ref, vstart, ostart):
    o, u = where_am_i()
    fill_starts(vir_ref, NV, vstart)
    fill_starts(occ_ref, NO, ostart)
    block = jnp.int32(0)
    for k in range(64):
        block += jnp.where(owner_ref[k] == u, k, 0)
    total = jnp.sum(parts_ref[...], axis=0)
    both = jnp.concatenate([total, pltpu.roll(total, 64, axis=1)], axis=0)
    wide = jnp.concatenate([both, jnp.zeros_like(both)], axis=1)
    lanes = lax.broadcasted_iota(jnp.int32, (8, 256), 1)
    row = lax.broadcasted_iota(jnp.int32, (8, 256), 0)
    column = jnp.where(row >= 4, SPAN - 4, 0) + block * 4 + row
    second = column >= NV
    sym = irrep_of(jnp.where(second, column - NV, column), vstart)
    sym = sym ^ jnp.where(second, vir_ref[1], vir_ref[0])
    result = jnp.zeros((8, 256), jnp.float32)
    for i in range(ROWS_I):
        mine = sym ^ occ_ref[o * ROWS_I + i]
        for g in range(IRREPS):
            begin = i * NO + ostart[g]
            end = i * NO + ostart[g + 1]
            moved = pltpu.roll(wide, begin - i * RUN_O, axis=1)
            here = (mine == g) & (lanes >= begin) & (lanes < end)
            result = jnp.where(here, moved, result)
    out_ref[...] = result[:, : ROWS_I * NO]


def finish(where_am_i, parts, occ_irrep, vir_irrep, owner):
    smem = pl.BlockSpec(memory_space=pltpu.SMEM)
    vmem = pl.BlockSpec(memory_space=pltpu.VMEM)
    return pl.pallas_call(
        functools.partial(finish_kernel, where_am_i),
        in_specs=[smem, smem, smem, vmem],
        out_specs=vmem,
        out_shape=jax.ShapeDtypeStruct((8, ROWS_I * NO), jnp.float32),
        scratch_shapes=[
            pltpu.SMEM((IRREPS + 1,), jnp.int32),
            pltpu.SMEM((IRREPS + 1,), jnp.int32),
        ],
        name="finish",
    )(vir_irrep, occ_irrep, owner, parts)


def shards(amplitudes, singles, integrals, occ_irrep, vir_irrep, owner):
    turned = jnp.transpose(integrals, (0, 2, 1))
    packed, high, low = pack(placed, amplitudes, singles, turned, occ_irrep, vir_irrep)
    everywhere = jnp.broadcast_to(packed[None], (8,) + packed.shape)
    gathered = lax.all_to_all(everywhere, "occ", 0, 0, tiled=True)
    mine = ladder(gathered, high, low, vir_irrep, owner)
    parts = lax.all_to_all(mine, "vir", 0, 0, tiled=True)
    return jnp.transpose(finish(placed, parts, occ_irrep, vir_irrep, owner))


def solution(mesh):
    specs = (P("occ", "vir"), P(), P(None, "vir", "occ"), P(), P(), P())
    return jax.shard_map(
        shards, mesh=mesh, in_specs=specs, out_specs=P("occ", "vir"), check_vma=False
    )
```

time: 672 us -> 93.5 us (0.14)
  waiting for transfers between devices: 626 us -> 0 us
  blocking collectives: 0 us -> 69.4 us
  Pallas kernels: 0 us -> 18.3 us
  matrix products: 15.7 us -> 0 us
  between operations: 14 us -> 0.04 us
    unnamed x4 -> x0, waiting for transfers between devices: 523 us -> none
    all_gather x2 -> x0, waiting for transfers between devices: 103 us -> none  [shards(): lax.all_gather(integrals[span_index], 'occ', axis=1, tiled=True)]
    all_to_all x0 -> x2, blocking collectives: none -> 69.4 us  [the longest x1 41 us: shards(): parts = lax.all_to_all(mine, 'vir', 0, 0, tiled=True)]
    pallas_call x0 -> x3, Pallas kernels: none -> 18.3 us  [the longest x1 13.5 us: pack(): pl.pallas_call(functools.partial(pack_kernel, where_am_i), grid=(1,), in_...]
    dot_general x4 -> x0, matrix products: 15.7 us -> none  [the longest x2 10.8 us: shards(): jnp.dot(tau_rows, lax.all_gather(integrals[span_index], 'occ', axis=1, ti...]
  transfers between devices with their start and end apart: 3 -> 0, of which waited for: 3 -> 0; matrix products, arithmetic and copies ran while one was open for 3% -> 0% of each run, Pallas kernels for 0% -> 0%
where the time goes in v1:
time: 93.5 us; the launch traced here: 93.2 us
  blocking collectives  69.4 us (74%)
  Pallas kernels  18.3 us (20%)
  local copies, waits for them, and re-layouts  5.41 us (6%)
    all_to_all x1, blocking collectives, shards(): parts = lax.all_to_all(mine, 'vir', 0, 0, tiled=True)  41 us
    all_to_all x1, blocking collectives, shards(): gathered = lax.all_to_all(everywhere, 'occ', 0, 0, tiled=True)  28.4 us
    pallas_call x1, Pallas kernels, pack(): pl.pallas_call(functools.partial(pack_kernel, where_am_i), grid=(1,), in_...  13.5 us
    unnamed x12, local copies, waits for them, and re-layouts  5.26 us
    pallas_call x1, Pallas kernels, ladder(): pl.pallas_call(ladder_kernel, in_specs=[smem, smem, vmem, vmem, vmem], ou...  2.66 us
    pallas_call x1, Pallas kernels, finish(): pl.pallas_call(functools.partial(finish_kernel, where_am_i), in_specs=[sm...  2.1 us

profile of v1, /device:TPU:1, one launch (start us, length us, event | category | flops | bytes accessed | tf_op | source)
XLA Modules:
  0.0 93.2 jit_solution(4867050340765607156)
XLA Ops:
  0.0 0.0 copy-start
  0.0 1.8 %copy-done = f32[200,3600]{1,0:T(8,128)S(1)} copy-done((f32[200,3600]{1,0:T(8,128)S(1)}, f32[200,3600]{1,0:T(8,128)}, u32[]{:S(2)}) %copy-start) | copy-done | bytes 2880024
  1.8 0.0 copy-start.1
  1.8 1.2 %copy-done.1 = f32[2,3600,32]{1,2,0:T(8,128)S(1)} copy-done((f32[2,3600,32]{1,2,0:T(8,128)S(1)}, f32[2,3600,32]{1,2,0:T(8,128)}, u32[]{:S(2)}) %copy-start.1) | copy-done | bytes 921624
  3.0 0.0 copy-start.2
  3.0 0.9 copy-done.2
  3.9 0.0 copy-start.3
  3.9 0.7 copy-done.3
  4.6 0.0 copy-start.5
  4.6 0.7 copy-done.5
  5.3 13.5 %pack.1 = (f32[32,1920]{1,0:T(8,128)S(1)}, bf16[512,1024]{1,0:T(8,128)(2,1)S(1)}, bf16[512,1024]{1,0:T(8,128)(2,1)S(1)}) custom-call(s32[480]{0:T(512)S(1)} %copy-done.3, s32[40]{0:T(128)S(1)} %copy-done.5, f32[200,3600]{1,0:T(8,128)S(1)} %copy-done, f32[200,3600]{1,0:T(8,128)S(1)} %copy-done, f32[2,32,3600]{2,1,0:T(8,128)S(1)} %bitcast.2, ...), custom_call_target="tpu_custom_call" | custom-call | tf_op jit(solution)/shard_map/pack/pallas_call | solution.py:222
  18.8 0.2 broadcast_in_dim.2
  18.9 0.0 copy-start.4
  18.9 28.4 %all_to_all.10.packed_ref = f32[8,32,1920]{2,1,0:T(8,128)S(1)} all-to-all(f32[8,32,1920]{2,1,0:T(8,128)S(1)} %broadcast_in_dim.2), channel_id=1, replica_groups=mesh['occ'=8,'vir'=64] {'occ'}, dimensions={0} | all-to-all | bytes 3932160 | tf_op jit(solution)/shard_map/all_to_all | solution.py:361
  47.4 0.0 copy-done.4
  47.4 2.7 %ladder.1 = f32[64,4,128]{2,1,0:T(4,128)S(1)} custom-call(s32[480]{0:T(512)S(1)} %copy-done.3, s32[64]{0:T(128)S(1)} %copy-done.4, f32[8,32,1920]{2,1,0:T(8,128)S(1)} %all_to_all.10.packed_ref, bf16[512,1024]{1,0:T(8,128)(2,1)S(1)} %get-tuple-element.9.high_ref, bf16[512,1024]{1,0:T(8,128)(2,1)S(1)} %get-tuple-element.10.low_ref), custom_call_target="tpu_custom_call" | custom-call | tf_op jit(solution)/shard_map/ladder/pallas_call | solution.py:298
  50.0 41.0 %all_to_all.11.parts_ref = f32[64,4,128]{2,1,0:T(4,128)} all-to-all(f32[64,4,128]{2,1,0:T(4,128)S(1)} %ladder.1), channel_id=1, replica_groups=mesh['occ'=8,'vir'=64] {'vir'}, dimensions={0} | all-to-all | bytes 262144 | tf_op jit(solution)/shard_map/all_to_all | solution.py:363
  91.1 2.1 %finish.1 = f32[8,200]{1,0:T(8,128)} custom-call(s32[480]{0:T(512)} %vir_ref.5, s32[40]{0:T(128)} %occ_ref.3, s32[64]{0:T(128)} %owner_ref.3, f32[64,4,128]{2,1,0:T(4,128)} %all_to_all.11.parts_ref), custom_call_target="tpu_custom_call" | custom-call | tf_op jit(solution)/shard_map/finish/pallas_call | solution.py:344
Async XLA Ops:
  0.0 1.8 %copy-start = (f32[200,3600]{1,0:T(8,128)S(1)}, f32[200,3600]{1,0:T(8,128)}, u32[]{:S(2)}) copy-start(f32[200,3600]{1,0:T(8,128)} %amp_tail.1) | copy-start | bytes 8640004
  1.8 1.2 %copy-start.1 = (f32[2,3600,32]{1,2,0:T(8,128)S(1)}, f32[2,3600,32]{1,2,0:T(8,128)}, u32[]{:S(2)}) copy-start(f32[2,3600,32]{1,2,0:T(8,128)} %param.8) | copy-start | bytes 2764804
  3.0 0.9 copy-start.2
  3.9 0.7 copy-start.3
  4.6 0.7 copy-start.5
  18.9 28.4 %copy-start.4 = (s32[64]{0:T(128)S(1)}, s32[64]{0:T(128)}, u32[]{:S(2)}) copy-start(s32[64]{0:T(128)} %owner_ref.3) | copy-start | bytes 772

commit v2 on v0

v2 whole, which is shorter than its diff:
```python
import functools

import jax
import jax.numpy as jnp
from jax import lax
from jax.experimental import pallas as pl
from jax.experimental.pallas import tpu as pltpu
from jax.sharding import PartitionSpec as P

NO = 40
NV = 480
SPAN = 256
IRREPS = 8
RUN_V = 120
RUN_O = 10
ROWS_I = 5
COLS = 32
CD = 3600
SLOTS = 8
LEAD = 256
WIDE = 33 * 128
MAIN = 28 * 128
GROUP = 64
PACK = 2 * SLOTS * RUN_V
ALL_VMEM = 64 * 1024 * 1024
HALF_VMEM = 32 * 1024 * 1024
FULL = 7 * 128
HALF = 64


def placed():
    return lax.axis_index("occ"), lax.axis_index("vir")


def fill_starts(labels, length, starts):
    bit = 1
    while bit * 2 <= length:
        bit *= 2
    low = [jnp.int32(0)] * IRREPS
    while bit:
        for g in range(1, IRREPS):
            cand = low[g] + bit
            below = labels[jnp.minimum(cand, length) - 1] < g
            low[g] = jnp.where((cand <= length) & below, cand, low[g])
        bit //= 2
    for g in range(IRREPS):
        starts[g] = low[g]
    starts[IRREPS] = jnp.int32(length)
    return low


def irrep_of(index, low):
    total = jnp.zeros_like(index)
    for g in range(1, IRREPS):
        total += (index >= low[g]).astype(jnp.int32)
    return total


def turn(near, far, position, inner, lanes):
    shift = lax.rem(position, 128)
    amount = lax.rem(inner + 128 - shift, 128)
    return pltpu.roll(jnp.where(lanes >= shift, near, far), amount, axis=1)


def inner_of(slot):
    return slot * RUN_V % 128


def tiles_of(turned, lanes):
    for slot in range(SLOTS - 1):
        yield jnp.where(lanes < inner_of(slot + 1), turned[slot], turned[slot + 1])
    yield turned[SLOTS - 1]


def first_pair(v):
    return (v * 15) // 2, (v % 2) * (NV // 2)


def pack_kernel(where_am_i, vir_hbm, int_hbm, out_hbm, labels, starts, ints, whole, packed, sems):
    copies = [
        pltpu.make_async_copy(vir_hbm, labels, sems.at[0]),
        pltpu.make_async_copy(
            int_hbm.at[:, :, pl.ds(0, MAIN)], ints.at[:, :, pl.ds(LEAD, MAIN)], sems.at[1]
        ),
        pltpu.make_async_copy(int_hbm, whole, sems.at[2]),
    ]
    for copy in copies:
        copy.start()
    o, v = where_am_i()
    c_first, offset = first_pair(v)
    rest = WIDE - LEAD - MAIN - 128
    ints[:, :, pl.ds(0, LEAD)] = jnp.zeros((2, COLS, LEAD), jnp.float32)
    ints[:, :, pl.ds(LEAD + MAIN, 128)] = jnp.zeros((2, COLS, 128), jnp.float32)
    ints[:, :, pl.ds(LEAD + MAIN + 128, rest)] = jnp.zeros((2, COLS, rest), jnp.float32)
    copies[0].wait()
    low = fill_starts(labels, NV, starts)
    copies[1].wait()
    copies[2].wait()
    ints[:, :, pl.ds(LEAD + MAIN, CD - MAIN)] = whole[:, :, pl.ds(MAIN, CD - MAIN)]

    lanes = lax.broadcasted_iota(jnp.int32, (COLS, 128), 1)
    row = lax.broadcasted_iota(jnp.int32, (COLS, 128), 0)
    sends = []

    def send(at, size):
        for n in range(8):
            copy = pltpu.make_async_copy(
                packed.at[:, pl.ds(at, size)],
                out_hbm.at[n, :, pl.ds(at, size)],
                sems.at[3 + len(sends)],
            )
            copy.start()
            sends.append(copy)

    held = None
    for s in range(2):
        first = s * SPAN + o * COLS
        a = (first >= NV).astype(jnp.int32)
        b = first - a * NV
        irr_a = labels[a]
        irr_b = irrep_of(row + b, low)
        turned = []
        for slot in range(SLOTS):
            cross = labels[c_first + slot] ^ irr_a
            value = jnp.zeros((COLS, 128), jnp.float32)
            for h in range(IRREPS):
                position = LEAD + slot * NV + starts[cross ^ h] - offset
                base = pl.multiple_of((position // 128) * 128, 128)
                near = ints[s, :, pl.ds(base, 128)]
                far = ints[s, :, pl.ds(base + 128, 128)]
                moved = turn(near, far, position, inner_of(slot), lanes)
                value = jnp.where(irr_b == h, moved, value)
            turned.append(value)
        tiles = list(tiles_of(turned, lanes))
        at = s * (FULL + 128)
        for t in range(7):
            packed[:, pl.ds(at + t * 128, 128)] = tiles[t]
        if s == 0:
            held = tiles[7]
            send(0, FULL)
        else:
            packed[:, pl.ds(FULL, 128)] = jnp.where(
                lanes < HALF, held, pltpu.roll(tiles[7], HALF, axis=1)
            )
            send(FULL, FULL + 128)
    for copy in sends:
        copy.wait()


def pack(where_am_i, integrals_t, vir_irrep):
    anywhere = pl.BlockSpec(memory_space=pl.ANY)
    return pl.pallas_call(
        functools.partial(pack_kernel, where_am_i),
        in_specs=[anywhere, anywhere],
        out_specs=anywhere,
        out_shape=jax.ShapeDtypeStruct((8, COLS, PACK), jnp.float32),
        scratch_shapes=[
            pltpu.SMEM((NV,), jnp.int32),
            pltpu.SMEM((IRREPS + 1,), jnp.int32),
            pltpu.VMEM((2, COLS, WIDE), jnp.float32),
            pltpu.VMEM((2, COLS, CD), jnp.float32),
            pltpu.VMEM((COLS, PACK), jnp.float32),
            pltpu.SemaphoreType.DMA((3 + 16,)),
        ],
        compiler_params=pltpu.CompilerParams(vmem_limit_bytes=ALL_VMEM),
        name="pack",
    )(vir_irrep, integrals_t)


def pack_tau(o, v, vir_ref, occ_ref, vstart, ostart, amp_ref, singles_ref, amps, ones, single_win, left, group, high, low):
    c_first, offset = first_pair(v)
    for t in range(CD // 128 + 1):
        size = min(128, CD - t * 128)
        amps[LEAD // 128 + t, pl.ds(0, ROWS_I * NO), pl.ds(0, size)] = amp_ref[:, pl.ds(t * 128, size)]
    amps[:, pl.ds(ROWS_I * NO, 16), :] = jnp.zeros((WIDE // 128, 16, 128), jnp.float32)

    ones[...] = jnp.zeros_like(ones)
    for t in range(4):
        size = min(128, NV - t * 128)
        ones[t, pl.ds(0, NO), pl.ds(0, size)] = singles_ref[:, pl.ds(t * 128, size)]
    lanes_w = lax.broadcasted_iota(jnp.int32, (16, 128), 1)
    for g in range(IRREPS):
        at, rows = vstart[g], pl.ds(ostart[g], 16)
        single_win[g] = turn(ones[at // 128, rows, :], ones[at // 128 + 1, rows, :], at, 0, lanes_w)
    lane_c = lax.broadcasted_iota(jnp.int32, (8, 128), 1)
    row_i = lax.broadcasted_iota(jnp.int32, (8, 1), 0)
    irr_i = [occ_ref[o * ROWS_I + i] for i in range(ROWS_I)]
    for slot in range(SLOTS):
        c = c_first + slot
        irr_c = vir_ref[c]
        own = ones[c // 128, pl.ds(o * ROWS_I, 8), :]
        column = jnp.sum(jnp.where(lane_c == lax.rem(c, 128), own, 0.0), axis=1, keepdims=True)
        for i in range(ROWS_I):
            column = jnp.where((row_i == i) & (irr_i[i] != irr_c), 0.0, column)
        left[slot] = jnp.broadcast_to(column, (8, 128))

    lanes = lax.broadcasted_iota(jnp.int32, (RUN_O, 128), 1)
    group[...] = jnp.zeros_like(group)

    def symmetry(sym, carry):
        turned = [[] for _ in range(ROWS_I)]
        for slot in range(SLOTS):
            g = vir_ref[c_first + slot] ^ sym
            begin = slot * NV + vstart[g] - offset
            from_lane = jnp.maximum(0, -begin)
            to_lane = jnp.minimum(vstart[g + 1] - vstart[g], CD - begin)
            inner = inner_of(slot)
            k = (lanes + (128 - inner)) & 127
            keep = (k >= from_lane) & (k < to_lane)
            near = (LEAD + begin) // 128
            right = pltpu.roll(single_win[g], inner, axis=1)[:RUN_O]
            for i in range(ROWS_I):
                rows = pl.ds(i * NO + ostart[irr_i[i] ^ sym], RUN_O)
                value = turn(amps[near, rows, :], amps[near + 1, rows, :], LEAD + begin, inner, lanes)
                product = left[slot, pl.ds(i, 1), :] * right
                turned[i].append(jnp.where(keep, value + product, 0.0))
        for i in range(ROWS_I):
            for t, tile in enumerate(tiles_of(turned[i], lanes)):
                if t == 7:
                    tile = jnp.where(lanes < HALF, tile, 0.0)
                group[pl.ds(i * RUN_O, RUN_O), pl.ds(t * 128, 128)] = tile
        tau = group[...]
        top = tau.astype(jnp.bfloat16)
        out = pl.ds(pl.multiple_of(sym * GROUP, GROUP), GROUP)
        high[out, :] = top
        low[out, :] = (tau - top.astype(jnp.float32)).astype(jnp.bfloat16)
        return carry

    lax.fori_loop(0, IRREPS, symmetry, 0)


def spread_index(o, u, vir_ref, occ_ref, owner_ref, vlow, olow):
    block = jnp.int32(0)
    for k in range(64):
        block += jnp.where(owner_ref[k] == u, k, 0)
    lanes = lax.broadcasted_iota(jnp.int32, (8, 256), 1)
    row = lax.broadcasted_iota(jnp.int32, (8, 256), 0)
    column = jnp.where(row >= 4, SPAN - 4, 0) + block * 4 + row
    second = column >= NV
    sym = irrep_of(jnp.where(second, column - NV, column), vlow)
    sym = sym ^ jnp.where(second, vir_ref[1], vir_ref[0])
    i = jnp.zeros_like(lanes)
    irr_i = jnp.zeros_like(lanes)
    for n in range(ROWS_I):
        i = jnp.where(lanes >= n * NO, n, i)
        irr_i = jnp.where(lanes >= n * NO, occ_ref[o * ROWS_I + n], irr_i)
    j = lanes - i * NO
    irr_j = irrep_of(j, olow)
    begin = jnp.zeros_like(lanes)
    for g in range(1, IRREPS):
        begin = jnp.where(irr_j == g, olow[g], begin)
    lane = i * RUN_O + j - begin + jnp.where(row >= 4, HALF, 0)
    return jnp.where((sym ^ irr_i ^ irr_j) == 0, lane, -1)


def ladder_kernel(
    where_am_i,
    vir_ref,
    occ_ref,
    owner_ref,
    packed_ref,
    amp_ref,
    singles_ref,
    out_ref,
    index_ref,
    vstart,
    ostart,
    amps,
    ones,
    single_win,
    left,
    group,
    high,
    low,
    top,
    bottom,
):
    o, v = where_am_i()
    vlow = fill_starts(vir_ref, NV, vstart)
    olow = fill_starts(occ_ref, NO, ostart)
    pack_tau(o, v, vir_ref, occ_ref, vstart, ostart, amp_ref, singles_ref, amps, ones, single_win, left, group, high, low)
    index_ref[...] = spread_index(o, v, vir_ref, occ_ref, owner_ref, vlow, olow)
    for source in range(8):
        for s in range(2):
            wide = packed_ref[source, :, pl.ds(s * (FULL + 128), FULL)]
            last = packed_ref[source, :, pl.ds(FULL, 128)]
            if s == 1:
                last = pltpu.roll(last, HALF, axis=1)
            rows = pl.ds(s * SPAN + source * COLS, COLS)
            for part, at, size in ((wide, 0, FULL), (last, FULL, 128)):
                upper = part.astype(jnp.bfloat16)
                top[rows, pl.ds(at, size)] = upper
                bottom[rows, pl.ds(at, size)] = (part - upper.astype(jnp.float32)).astype(jnp.bfloat16)
    contract = functools.partial(
        lax.dot_general,
        dimension_numbers=(((1,), (1,)), ((), ())),
        preferred_element_type=jnp.float32,
    )
    upper, lower = top[...], bottom[...]
    sums = contract(upper, high[...]) + contract(lower, high[...]) + contract(upper, low[...])
    column = lax.broadcasted_iota(jnp.int32, (2 * SPAN, 128), 0)
    second = column >= NV
    sym = irrep_of(jnp.where(second, column - NV, column), vlow)
    sym = sym ^ jnp.where(second, vir_ref[1], vir_ref[0])
    pair = sym >> 1
    picked = sums[:, 0:128]
    for t in range(1, 4):
        picked = jnp.where(pair == t, sums[:, t * 128 : (t + 1) * 128], picked)
    span = (column >= SPAN).astype(jnp.int32)
    picked = jnp.where((sym & 1) == span, picked, pltpu.roll(picked, HALF, axis=1))
    lanes = lax.broadcasted_iota(jnp.int32, (SPAN, 128), 1)
    both = 0.5 * jnp.where(lanes < HALF, picked[:SPAN], picked[SPAN:])
    for k in range(64):
        out_ref[owner_ref[k]] = both[4 * k : 4 * k + 4, :]


def ladder(where_am_i, packed, amplitudes, singles, occ_irrep, vir_irrep, owner):
    smem = pl.BlockSpec(memory_space=pltpu.SMEM)
    vmem = pl.BlockSpec(memory_space=pltpu.VMEM)
    depth = SLOTS * 128
    return pl.pallas_call(
        functools.partial(ladder_kernel, where_am_i),
        in_specs=[smem, smem, smem, vmem, vmem, vmem],
        out_specs=[vmem, vmem],
        out_shape=[
            jax.ShapeDtypeStruct((64, 4, 128), jnp.float32),
            jax.ShapeDtypeStruct((8, 256), jnp.int32),
        ],
        scratch_shapes=[
            pltpu.SMEM((IRREPS + 1,), jnp.int32),
            pltpu.SMEM((IRREPS + 1,), jnp.int32),
            pltpu.VMEM((WIDE // 128, ROWS_I * NO + 16, 128), jnp.float32),
            pltpu.VMEM((5, NO + 16, 128), jnp.float32),
            pltpu.VMEM((IRREPS, 16, 128), jnp.float32),
            pltpu.VMEM((SLOTS, 8, 128), jnp.float32),
            pltpu.VMEM((GROUP, depth), jnp.float32),
            pltpu.VMEM((IRREPS * GROUP, depth), jnp.bfloat16),
            pltpu.VMEM((IRREPS * GROUP, depth), jnp.bfloat16),
            pltpu.VMEM((2 * SPAN, depth), jnp.bfloat16),
            pltpu.VMEM((2 * SPAN, depth), jnp.bfloat16),
        ],
        compiler_params=pltpu.CompilerParams(vmem_limit_bytes=HALF_VMEM),
        name="ladder",
    )(vir_irrep, occ_irrep, owner, packed, amplitudes, singles)


def finish_kernel(parts_ref, index_ref, out_ref):
    total = jnp.sum(parts_ref[...], axis=0)
    both = jnp.concatenate([total, total], axis=0)
    index = index_ref[...]
    lane = jnp.maximum(index, 0)
    near = jnp.take_along_axis(both, lane[:, :128], axis=1)
    far = jnp.take_along_axis(both, lane[:, 128:], axis=1)
    result = jnp.where(index >= 0, jnp.concatenate([near, far], axis=1), 0.0)
    out_ref[...] = result[:, : ROWS_I * NO]


def finish(parts, index):
    vmem = pl.BlockSpec(memory_space=pltpu.VMEM)
    return pl.pallas_call(
        finish_kernel,
        in_specs=[vmem, vmem],
        out_specs=vmem,
        out_shape=jax.ShapeDtypeStruct((8, ROWS_I * NO), jnp.float32),
        name="finish",
    )(parts, index)


def shards(amplitudes, singles, integrals, occ_irrep, vir_irrep, owner):
    packed = pack(placed, jnp.transpose(integrals, (0, 2, 1)), vir_irrep)
    gathered = lax.all_to_all(packed, "occ", 0, 0, tiled=True)
    mine, index = ladder(placed, gathered, amplitudes, singles, occ_irrep, vir_irrep, owner)
    parts = lax.all_to_all(mine, "vir", 0, 0, tiled=True)
    return jnp.transpose(finish(parts, index))


def solution(mesh):
    specs = (P("occ", "vir"), P(), P(None, "vir", "occ"), P(), P(), P())
    return jax.shard_map(
        shards, mesh=mesh, in_specs=specs, out_specs=P("occ", "vir"), check_vma=False
    )
```

time: 672 us -> 80.1 us (0.12)
  waiting for transfers between devices: 626 us -> 0 us
  blocking collectives: 0 us -> 69.3 us
  matrix products: 15.7 us -> 0 us
  between operations: 14 us -> 0.08 us
  local copies, waits for them, and re-layouts: 10.7 us -> 0.04 us
  Pallas kernels: 0 us -> 10.5 us
    unnamed x4 -> x0, waiting for transfers between devices: 523 us -> none
    all_gather x2 -> x0, waiting for transfers between devices: 103 us -> none  [shards(): lax.all_gather(integrals[span_index], 'occ', axis=1, tiled=True)]
    all_to_all x0 -> x2, blocking collectives: none -> 69.3 us  [the longest x1 42.4 us: shards(): parts = lax.all_to_all(mine, 'vir', 0, 0, tiled=True)]
    dot_general x4 -> x0, matrix products: 15.7 us -> none  [the longest x2 10.8 us: shards(): jnp.dot(tau_rows, lax.all_gather(integrals[span_index], 'occ', axis=1, ti...]
    pallas_call x0 -> x3, Pallas kernels: none -> 10.5 us  [the longest x1 4.97 us: ladder(): pl.pallas_call(functools.partial(ladder_kernel, where_am_i), in_specs=[sm...]
  transfers between devices with their start and end apart: 3 -> 0, of which waited for: 3 -> 0; matrix products, arithmetic and copies ran while one was open for 3% -> 0% of each run, Pallas kernels for 0% -> 0%
where the time goes in v2:
time: 80.1 us; the launch traced here: 79.9 us
  blocking collectives  69.3 us (87%)
  Pallas kernels  10.5 us (13%)
    all_to_all x1, blocking collectives, shards(): parts = lax.all_to_all(mine, 'vir', 0, 0, tiled=True)  42.4 us
    all_to_all x1, blocking collectives, shards(): gathered = lax.all_to_all(packed, 'occ', 0, 0, tiled=True)  26.9 us
    pallas_call x1, Pallas kernels, ladder(): pl.pallas_call(functools.partial(ladder_kernel, where_am_i), in_specs=[sm...  4.97 us
    pallas_call x1, Pallas kernels, pack(): pl.pallas_call(functools.partial(pack_kernel, where_am_i), in_specs=[anyw...  3.84 us
    pallas_call x1, Pallas kernels, finish(): pl.pallas_call(finish_kernel, in_specs=[vmem, vmem], out_specs=vmem, out_...  1.65 us

profile of v2, /device:TPU:1, one launch (start us, length us, event | category | flops | bytes accessed | tf_op | source)
XLA Modules:
  0.0 79.9 jit_solution(1931028334711801332)
XLA Ops:
  0.0 3.8 %pack.1 = f32[8,32,1920]{2,1,0:T(8,128)} custom-call(s32[480]{0:T(512)} %vir_ref.1, f32[2,32,3600]{2,1,0:T(8,128)} %bitcast.2), custom_call_target="tpu_custom_call" | custom-call | tf_op jit(solution)/shard_map/pack/pallas_call | solution.py:152
  3.8 0.0 copy-start
  3.9 0.0 copy-start.1
  3.9 0.0 copy-start.2
  3.9 0.0 copy-start.4
  3.9 0.0 copy-start.5
  3.9 26.9 %all_to_all.10.packed_ref = f32[8,32,1920]{2,1,0:T(8,128)S(1)} all-to-all(f32[8,32,1920]{2,1,0:T(8,128)} %pack.1), channel_id=1, replica_groups=mesh['occ'=8,'vir'=64] {'occ'}, dimensions={0} | all-to-all | bytes 3932160 | tf_op jit(solution)/shard_map/all_to_all | solution.py:371
  30.8 0.0 copy-done
  30.8 0.0 copy-done.1
  30.8 0.0 copy-done.2
  30.8 0.0 copy-done.4
  30.8 0.0 copy-done.5
  30.8 5.0 %ladder.1 = (f32[64,4,128]{2,1,0:T(4,128)S(1)}, s32[8,256]{1,0:T(8,128)S(1)}) custom-call(s32[480]{0:T(512)S(1)} %copy-done.2, s32[40]{0:T(128)S(1)} %copy-done.4, s32[64]{0:T(128)S(1)} %copy-done.5, f32[8,32,1920]{2,1,0:T(8,128)S(1)} %all_to_all.10.packed_ref, f32[200,3600]{1,0:T(8,128)S(1)} %copy-done, f32[40,480]{1,0:T(8,128)S(1)} %copy-done.1), custom_call_target="tpu_custom_call" | custom-call | tf_op jit(solution)/shard_map/ladder/pallas_call | solution.py:321
  35.8 0.0 copy-start.3
  35.8 42.4 %all_to_all.11.parts_ref = f32[64,4,128]{2,1,0:T(4,128)} all-to-all(f32[64,4,128]{2,1,0:T(4,128)S(1)} %get-tuple-element.7), channel_id=1, replica_groups=mesh['occ'=8,'vir'=64] {'vir'}, dimensions={0} | all-to-all | bytes 262144 | tf_op jit(solution)/shard_map/all_to_all | solution.py:373
  78.2 0.0 copy-done.3
  78.2 1.6 %finish.1 = f32[8,200]{1,0:T(8,128)} custom-call(f32[64,4,128]{2,1,0:T(4,128)} %all_to_all.11.parts_ref, s32[8,256]{1,0:T(8,128)} %copy-done.3), custom_call_target="tpu_custom_call" | custom-call | tf_op jit(solution)/shard_map/finish/pallas_call | solution.py:360
Async XLA Ops:
  3.8 26.9 %copy-start = (f32[200,3600]{1,0:T(8,128)S(1)}, f32[200,3600]{1,0:T(8,128)}, u32[]{:S(2)}) copy-start(f32[200,3600]{1,0:T(8,128)} %amp_ref.1) | copy-start | bytes 8640004
  3.9 26.9 %copy-start.1 = (f32[40,480]{1,0:T(8,128)S(1)}, f32[40,480]{1,0:T(8,128)}, u32[]{:S(2)}) copy-start(f32[40,480]{1,0:T(8,128)} %singles_ref.1) | copy-start | bytes 230404
  3.9 26.9 %copy-start.2 = (s32[480]{0:T(512)S(1)}, s32[480]{0:T(512)}, u32[]{:S(2)}) copy-start(s32[480]{0:T(512)} %vir_ref.1) | copy-start | bytes 5764
  3.9 26.9 %copy-start.4 = (s32[40]{0:T(128)S(1)}, s32[40]{0:T(128)}, u32[]{:S(2)}) copy-start(s32[40]{0:T(128)} %occ_ref.1) | copy-start | bytes 484
  3.9 26.9 %copy-start.5 = (s32[64]{0:T(128)S(1)}, s32[64]{0:T(128)}, u32[]{:S(2)}) copy-start(s32[64]{0:T(128)} %owner_ref.1) | copy-start | bytes 772
  35.8 42.4 %copy-start.3 = (s32[8,256]{1,0:T(8,128)}, s32[8,256]{1,0:T(8,128)S(1)}, u32[]{:S(2)}) copy-start(s32[8,256]{1,0:T(8,128)S(1)} %get-tuple-element.8.index_ref) | copy-start | bytes 24580

commit v3 on v2

--- a/solution.py
+++ b/solution.py
@@ -23,7 +23,7 @@
 GROUP = 64
 PACK = 2 * SLOTS * RUN_V
 ALL_VMEM = 64 * 1024 * 1024
-HALF_VMEM = 32 * 1024 * 1024
+SOME_VMEM = 12 * 1024 * 1024
 FULL = 7 * 128
 HALF = 64
 
@@ -77,26 +77,30 @@
 
 
 def pack_kernel(where_am_i, vir_hbm, int_hbm, out_hbm, labels, starts, ints, whole, packed, sems):
-    copies = [
-        pltpu.make_async_copy(vir_hbm, labels, sems.at[0]),
-        pltpu.make_async_copy(
-            int_hbm.at[:, :, pl.ds(0, MAIN)], ints.at[:, :, pl.ds(LEAD, MAIN)], sems.at[1]
-        ),
-        pltpu.make_async_copy(int_hbm, whole, sems.at[2]),
-    ]
-    for copy in copies:
-        copy.start()
+    label_copy = pltpu.make_async_copy(vir_hbm, labels, sems.at[0])
+    label_copy.start()
+    copies = []
+    for s in range(2):
+        copies.append(
+            [
+                pltpu.make_async_copy(
+                    int_hbm.at[s, :, pl.ds(0, MAIN)],
+                    ints.at[s, :, pl.ds(LEAD, MAIN)],
+                    sems.at[1 + 2 * s],
+                ),
+                pltpu.make_async_copy(int_hbm.at[s], whole.at[s], sems.at[2 + 2 * s]),
+            ]
+        )
+        for copy in copies[s]:
+            copy.start()
     o, v = where_am_i()
     c_first, offset = first_pair(v)
     rest = WIDE - LEAD - MAIN - 128
     ints[:, :, pl.ds(0, LEAD)] = jnp.zeros((2, COLS, LEAD), jnp.float32)
     ints[:, :, pl.ds(LEAD + MAIN, 128)] = jnp.zeros((2, COLS, 128), jnp.float32)
     ints[:, :, pl.ds(LEAD + MAIN + 128, rest)] = jnp.zeros((2, COLS, rest), jnp.float32)
-    copies[0].wait()
+    label_copy.wait()
     low = fill_starts(labels, NV, starts)
-    copies[1].wait()
-    copies[2].wait()
-    ints[:, :, pl.ds(LEAD + MAIN, CD - MAIN)] = whole[:, :, pl.ds(MAIN, CD - MAIN)]
 
     lanes = lax.broadcasted_iota(jnp.int32, (COLS, 128), 1)
     row = lax.broadcasted_iota(jnp.int32, (COLS, 128), 0)
@@ -107,13 +111,16 @@
             copy = pltpu.make_async_copy(
                 packed.at[:, pl.ds(at, size)],
                 out_hbm.at[n, :, pl.ds(at, size)],
-                sems.at[3 + len(sends)],
+                sems.at[5 + len(sends)],
             )
             copy.start()
             sends.append(copy)
 
     held = None
     for s in range(2):
+        for copy in copies[s]:
+            copy.wait()
+        ints[s, :, pl.ds(LEAD + MAIN, CD - MAIN)] = whole[s, :, pl.ds(MAIN, CD - MAIN)]
         first = s * SPAN + o * COLS
         a = (first >= NV).astype(jnp.int32)
         b = first - a * NV
@@ -131,18 +138,21 @@
                 moved = turn(near, far, position, inner_of(slot), lanes)
                 value = jnp.where(irr_b == h, moved, value)
             turned.append(value)
-        tiles = list(tiles_of(turned, lanes))
-        at = s * (FULL + 128)
-        for t in range(7):
-            packed[:, pl.ds(at + t * 128, 128)] = tiles[t]
+            at = s * (FULL + 128)
+            if slot:
+                tile = jnp.where(lanes < inner_of(slot), turned[slot - 1], value)
+                packed[:, pl.ds(at + (slot - 1) * 128, 128)] = tile
+            if s == 1 and slot == 4:
+                send(FULL + 128, 4 * 128)
         if s == 0:
-            held = tiles[7]
+            held = turned[7]
             send(0, FULL)
         else:
             packed[:, pl.ds(FULL, 128)] = jnp.where(
-                lanes < HALF, held, pltpu.roll(tiles[7], HALF, axis=1)
+                lanes < HALF, held, pltpu.roll(turned[7], HALF, axis=1)
             )
-            send(FULL, FULL + 128)
+            send(FULL, 128)
+            send(FULL + 5 * 128, 3 * 128)
     for copy in sends:
         copy.wait()
 
@@ -160,7 +170,7 @@
             pltpu.VMEM((2, COLS, WIDE), jnp.float32),
             pltpu.VMEM((2, COLS, CD), jnp.float32),
             pltpu.VMEM((COLS, PACK), jnp.float32),
-            pltpu.SemaphoreType.DMA((3 + 16,)),
+            pltpu.SemaphoreType.DMA((5 + 32,)),
         ],
         compiler_params=pltpu.CompilerParams(vmem_limit_bytes=ALL_VMEM),
         name="pack",
@@ -253,15 +263,15 @@
     return jnp.where((sym ^ irr_i ^ irr_j) == 0, lane, -1)
 
 
-def ladder_kernel(
+def tau_kernel(
     where_am_i,
     vir_ref,
     occ_ref,
     owner_ref,
-    packed_ref,
     amp_ref,
     singles_ref,
-    out_ref,
+    high,
+    low,
     index_ref,
     vstart,
     ostart,
@@ -270,16 +280,44 @@
     single_win,
     left,
     group,
-    high,
-    low,
-    top,
-    bottom,
 ):
     o, v = where_am_i()
     vlow = fill_starts(vir_ref, NV, vstart)
     olow = fill_starts(occ_ref, NO, ostart)
     pack_tau(o, v, vir_ref, occ_ref, vstart, ostart, amp_ref, singles_ref, amps, ones, single_win, left, group, high, low)
     index_ref[...] = spread_index(o, v, vir_ref, occ_ref, owner_ref, vlow, olow)
+
+
+def tau(where_am_i, amplitudes, singles, occ_irrep, vir_irrep, owner):
+    smem = pl.BlockSpec(memory_space=pltpu.SMEM)
+    vmem = pl.BlockSpec(memory_space=pltpu.VMEM)
+    depth = SLOTS * 128
+    return pl.pallas_call(
+        functools.partial(tau_kernel, where_am_i),
+        in_specs=[smem, smem, smem, vmem, vmem],
+        out_specs=[vmem, vmem, vmem],
+        out_shape=[
+            jax.ShapeDtypeStruct((IRREPS * GROUP, depth), jnp.bfloat16),
+            jax.ShapeDtypeStruct((IRREPS * GROUP, depth), jnp.bfloat16),
+            jax.ShapeDtypeStruct((8, 256), jnp.int32),
+        ],
+        scratch_shapes=[
+            pltpu.SMEM((IRREPS + 1,), jnp.int32),
+            pltpu.SMEM((IRREPS + 1,), jnp.int32),
+            pltpu.VMEM((WIDE // 128, ROWS_I * NO + 16, 128), jnp.float32),
+            pltpu.VMEM((5, NO + 16, 128), jnp.float32),
+            pltpu.VMEM((IRREPS, 16, 128), jnp.float32),
+            pltpu.VMEM((SLOTS, 8, 128), jnp.float32),
+            pltpu.VMEM((GROUP, depth), jnp.float32),
+        ],
+        compiler_params=pltpu.CompilerParams(vmem_limit_bytes=SOME_VMEM),
+        cost_estimate=pl.CostEstimate(flops=0, bytes_accessed=8 * 1024 * 1024, transcendentals=0),
+        name="tau",
+    )(vir_irrep, occ_irrep, owner, amplitudes, singles)
+
+
+def ladder_kernel(vir_ref, owner_ref, packed_ref, high, low, out_ref, vstart, top, bottom):
+    vlow = fill_starts(vir_ref, NV, vstart)
     for source in range(8):
         for s in range(2):
             wide = packed_ref[source, :, pl.ds(s * (FULL + 128), FULL)]
@@ -314,34 +352,23 @@
         out_ref[owner_ref[k]] = both[4 * k : 4 * k + 4, :]
 
 
-def ladder(where_am_i, packed, amplitudes, singles, occ_irrep, vir_irrep, owner):
+def ladder(packed, high, low, vir_irrep, owner):
     smem = pl.BlockSpec(memory_space=pltpu.SMEM)
     vmem = pl.BlockSpec(memory_space=pltpu.VMEM)
     depth = SLOTS * 128
     return pl.pallas_call(
-        functools.partial(ladder_kernel, where_am_i),
-        in_specs=[smem, smem, smem, vmem, vmem, vmem],
-        out_specs=[vmem, vmem],
-        out_shape=[
-            jax.ShapeDtypeStruct((64, 4, 128), jnp.float32),
-            jax.ShapeDtypeStruct((8, 256), jnp.int32),
-        ],
+        ladder_kernel,
+        in_specs=[smem, smem, vmem, vmem, vmem],
+        out_specs=vmem,
+        out_shape=jax.ShapeDtypeStruct((64, 4, 128), jnp.float32),
         scratch_shapes=[
             pltpu.SMEM((IRREPS + 1,), jnp.int32),
-            pltpu.SMEM((IRREPS + 1,), jnp.int32),
-            pltpu.VMEM((WIDE // 128, ROWS_I * NO + 16, 128), jnp.float32),
-            pltpu.VMEM((5, NO + 16, 128), jnp.float32),
-            pltpu.VMEM((IRREPS, 16, 128), jnp.float32),
-            pltpu.VMEM((SLOTS, 8, 128), jnp.float32),
-            pltpu.VMEM((GROUP, depth), jnp.float32),
-            pltpu.VMEM((IRREPS * GROUP, depth), jnp.bfloat16),
-            pltpu.VMEM((IRREPS * GROUP, depth), jnp.bfloat16),
             pltpu.VMEM((2 * SPAN, depth), jnp.bfloat16),
             pltpu.VMEM((2 * SPAN, depth), jnp.bfloat16),
         ],
-        compiler_params=pltpu.CompilerParams(vmem_limit_bytes=HALF_VMEM),
+        compiler_params=pltpu.CompilerParams(vmem_limit_bytes=SOME_VMEM),
         name="ladder",
-    )(vir_irrep, occ_irrep, owner, packed, amplitudes, singles)
+    )(vir_irrep, owner, packed, high, low)
 
 
 def finish_kernel(parts_ref, index_ref, out_ref):
@@ -362,6 +389,7 @@
         in_specs=[vmem, vmem],
         out_specs=vmem,
         out_shape=jax.ShapeDtypeStruct((8, ROWS_I * NO), jnp.float32),
+        compiler_params=pltpu.CompilerParams(vmem_limit_bytes=1024 * 1024),
         name="finish",
     )(parts, index)
 
@@ -369,7 +397,8 @@
 def shards(amplitudes, singles, integrals, occ_irrep, vir_irrep, owner):
     packed = pack(placed, jnp.transpose(integrals, (0, 2, 1)), vir_irrep)
     gathered = lax.all_to_all(packed, "occ", 0, 0, tiled=True)
-    mine, index = ladder(placed, gathered, amplitudes, singles, occ_irrep, vir_irrep, owner)
+    high, low, index = tau(placed, amplitudes, singles, occ_irrep, vir_irrep, owner)
+    mine = ladder(gathered, high, low, vir_irrep, owner)
     parts = lax.all_to_all(mine, "vir", 0, 0, tiled=True)
     return jnp.transpose(finish(parts, index))
 

time: 80.1 us -> 76.6 us (0.956)
  blocking collectives: 69.3 us -> 38.1 us
  waiting for transfers between devices: 0 us -> 17.8 us
  starting transfers between devices: 0 us -> 6.09 us
  local copies, waits for them, and re-layouts: 0.04 us -> 4.07 us
    all_to_all x1 -> x0, blocking collectives: 26.9 us -> none  [shards(): gathered = lax.all_to_all(packed, 'occ', 0, 0, tiled=True)]
    all_to_all x0 -> x1, waiting for transfers between devices: none -> 17.8 us  [shards(): gathered = lax.all_to_all(packed, 'occ', 0, 0, tiled=True)]
    all_to_all x0 -> x1, starting transfers between devices: none -> 6.09 us  [shards(): gathered = lax.all_to_all(packed, 'occ', 0, 0, tiled=True)]
    all_to_all x1, blocking collectives: 42.4 us -> 38.1 us  [shards(): parts = lax.all_to_all(mine, 'vir', 0, 0, tiled=True)]
    unnamed x12 -> x14, local copies, waits for them, and re-layouts: 0.04 us -> 4.07 us
    pallas_call x1, Pallas kernels: 1.65 us -> 0.74 us  [finish(): pl.pallas_call(finish_kernel, in_specs=[vmem, vmem], out_specs=vmem, out_...]
    pallas_call x1 -> x2, Pallas kernels: 4.97 us -> 5.68 us  [the longest x1 3.07 us: tau(): pl.pallas_call(functools.partial(tau_kernel, where_am_i), in_specs=[smem,...]
  transfers between devices with their start and end apart: 0 -> 1, of which waited for: 0 -> 1; matrix products, arithmetic and copies ran while one was open for 0% -> 0% of each run, Pallas kernels for 0% -> 4%
where the time goes in v3:
time: 76.6 us; the launch traced here: 76.3 us
  blocking collectives  38.1 us (50%)
  waiting for transfers between devices  17.8 us (23%)
  Pallas kernels  10.2 us (13%)
  starting transfers between devices  6.09 us (8%)
  local copies, waits for them, and re-layouts  4.07 us (5%)
    all_to_all x1, blocking collectives, shards(): parts = lax.all_to_all(mine, 'vir', 0, 0, tiled=True)  38.1 us
    all_to_all x1, waiting for transfers between devices, shards(): gathered = lax.all_to_all(packed, 'occ', 0, 0, tiled=True)  17.8 us
    all_to_all x1, starting transfers between devices, shards(): gathered = lax.all_to_all(packed, 'occ', 0, 0, tiled=True)  6.09 us
    unnamed x14, local copies, waits for them, and re-layouts  4.07 us
    pallas_call x1, Pallas kernels, pack(): pl.pallas_call(functools.partial(pack_kernel, where_am_i), in_specs=[anyw...  3.77 us
    pallas_call x1, Pallas kernels, tau(): pl.pallas_call(functools.partial(tau_kernel, where_am_i), in_specs=[smem,...  3.07 us
    pallas_call x1, Pallas kernels, ladder(): pl.pallas_call(ladder_kernel, in_specs=[smem, smem, vmem, vmem, vmem], ou...  2.6 us
  transfers between devices with their start and end apart: 1, of which 1 were waited for; matrix products, arithmetic and copies ran while one was open for 0% of the time, Pallas kernels for 4%

profile of v3, /device:TPU:1, one launch (start us, length us, event | category | flops | bytes accessed | tf_op | source)
XLA Modules:
  0.0 76.3 jit_solution(3136370163725331175)
XLA Ops:
  0.0 3.8 %pack.1 = f32[8,32,1920]{2,1,0:T(8,128)} custom-call(s32[480]{0:T(512)} %vir_ref.3, f32[2,32,3600]{2,1,0:T(8,128)} %bitcast.2), custom_call_target="tpu_custom_call" | custom-call | tf_op jit(solution)/shard_map/pack/pallas_call | solution.py:162
  3.8 0.0 copy-start.3
  3.8 0.0 copy-start.4
  3.8 0.0 copy-start.5
  3.8 0.0 copy-start.6
  3.8 6.1 %all-to-all-start = ((f32[8,32,1920]{2,1,0:T(8,128)}), f32[8,32,1920]{2,1,0:T(8,128)S(1)}, u32[]{:S(2)}, u32[]{:S(2)}) async-start(f32[8,32,1920]{2,1,0:T(8,128)} %pack.1), calls=%async_computation | async-start | bytes 3932160 | tf_op jit(solution)/shard_map/all_to_all | solution.py:399
  9.9 0.0 copy-done.3
  9.9 0.0 copy-done.4
  9.9 0.0 copy-done.5
  9.9 0.0 copy-done.6
  10.0 0.0 copy-start
  10.0 1.8 %copy-done = f32[200,3600]{1,0:T(8,128)S(1)} copy-done((f32[200,3600]{1,0:T(8,128)S(1)}, f32[200,3600]{1,0:T(8,128)}, u32[]{:S(2)}) %copy-start) | copy-done | bytes 2880024
  11.8 3.1 %tau.1 = (bf16[512,1024]{1,0:T(8,128)(2,1)S(1)}, bf16[512,1024]{1,0:T(8,128)(2,1)S(1)}, s32[8,256]{1,0:T(8,128)S(1)}) custom-call(s32[480]{0:T(512)S(1)} %copy-done.4, s32[40]{0:T(128)S(1)} %copy-done.6, s32[64]{0:T(128)S(1)} %copy-done.5, f32[200,3600]{1,0:T(8,128)S(1)} %copy-done, f32[40,480]{1,0:T(8,128)S(1)} %copy-done.3), custom_call_target="tpu_custom_call" | custom-call | bytes 8388608 | tf_op jit(solution)/shard_map/tau/pallas_call | solution.py:295
  14.9 0.0 copy-start.1
  14.9 1.0 %copy-done.1 = bf16[512,1024]{1,0:T(8,128)(2,1)} copy-done((bf16[512,1024]{1,0:T(8,128)(2,1)}, bf16[512,1024]{1,0:T(8,128)(2,1)S(1)}, u32[]{:S(2)}) %copy-start.1) | copy-done | bytes 1048600
  15.9 17.8 %all-to-all-done.packed_ref = f32[8,32,1920]{2,1,0:T(8,128)S(1)} async-done(((f32[8,32,1920]{2,1,0:T(8,128)}), f32[8,32,1920]{2,1,0:T(8,128)S(1)}, u32[]{:S(2)}, u32[]{:S(2)}) %all-to-all-start) | async-done | bytes 1966112 | tf_op jit(solution)/shard_map/all_to_all | solution.py:399
  33.7 0.0 copy-start.2
  33.7 1.2 %copy-done.2 = bf16[512,1024]{1,0:T(8,128)(2,1)S(1)} copy-done((bf16[512,1024]{1,0:T(8,128)(2,1)S(1)}, bf16[512,1024]{1,0:T(8,128)(2,1)}, u32[]{:S(2)}) %copy-start.2) | copy-done | bytes 1048600
  34.9 2.6 %ladder.1 = f32[64,4,128]{2,1,0:T(4,128)S(1)} custom-call(s32[480]{0:T(512)S(1)} %copy-done.4, s32[64]{0:T(128)S(1)} %copy-done.5, f32[8,32,1920]{2,1,0:T(8,128)S(1)} %all-to-all-done.packed_ref, bf16[512,1024]{1,0:T(8,128)(2,1)S(1)} %get-tuple-element.8.high, bf16[512,1024]{1,0:T(8,128)(2,1)S(1)} %copy-done.2), custom_call_target="tpu_custom_call" | custom-call | tf_op jit(solution)/shard_map/ladder/pallas_call | solution.py:359
  37.5 38.1 %all_to_all.10.parts_ref = f32[64,4,128]{2,1,0:T(4,128)S(1)} all-to-all(f32[64,4,128]{2,1,0:T(4,128)S(1)} %ladder.1), channel_id=1, replica_groups=mesh['occ'=8,'vir'=64] {'vir'}, dimensions={0} | all-to-all | bytes 262144 | tf_op jit(solution)/shard_map/all_to_all | solution.py:402
  75.6 0.7 finish.1
Async XLA Ops:
  3.8 6.1 %copy-start.3 = (f32[40,480]{1,0:T(8,128)S(1)}, f32[40,480]{1,0:T(8,128)}, u32[]{:S(2)}) copy-start(f32[40,480]{1,0:T(8,128)} %singles_ref.1) | copy-start | bytes 230404
  3.8 6.1 %copy-start.4 = (s32[480]{0:T(512)S(1)}, s32[480]{0:T(512)}, u32[]{:S(2)}) copy-start(s32[480]{0:T(512)} %vir_ref.3) | copy-start | bytes 5764
  3.8 6.1 %copy-start.5 = (s32[64]{0:T(128)S(1)}, s32[64]{0:T(128)}, u32[]{:S(2)}) copy-start(s32[64]{0:T(128)} %owner_ref.3) | copy-start | bytes 772
  3.8 6.1 %copy-start.6 = (s32[40]{0:T(128)S(1)}, s32[40]{0:T(128)}, u32[]{:S(2)}) copy-start(s32[40]{0:T(128)} %occ_ref.1) | copy-start | bytes 484
  3.8 29.8 %all-to-all-start = ((f32[8,32,1920]{2,1,0:T(8,128)}), f32[8,32,1920]{2,1,0:T(8,128)S(1)}, u32[]{:S(2)}, u32[]{:S(2)}) async-start(f32[8,32,1920]{2,1,0:T(8,128)} %pack.1), calls=%async_computation | async-start | bytes 3932160 | tf_op jit(solution)/shard_map/all_to_all | solution.py:399
  10.0 1.8 %copy-start = (f32[200,3600]{1,0:T(8,128)S(1)}, f32[200,3600]{1,0:T(8,128)}, u32[]{:S(2)}) copy-start(f32[200,3600]{1,0:T(8,128)} %amp_ref.1) | copy-start | bytes 8640004
  14.9 1.0 %copy-start.1 = (bf16[512,1024]{1,0:T(8,128)(2,1)}, bf16[512,1024]{1,0:T(8,128)(2,1)S(1)}, u32[]{:S(2)}) copy-start(bf16[512,1024]{1,0:T(8,128)(2,1)S(1)} %get-tuple-element.9.low) | copy-start | bytes 3145732
  33.7 1.2 %copy-start.2 = (bf16[512,1024]{1,0:T(8,128)(2,1)S(1)}, bf16[512,1024]{1,0:T(8,128)(2,1)}, u32[]{:S(2)}) copy-start(bf16[512,1024]{1,0:T(8,128)(2,1)} %copy-done.1) | copy-start | bytes 3145732

commit v4 on v3

--- a/solution.py
+++ b/solution.py
@@ -20,7 +20,7 @@
 LEAD = 256
 WIDE = 33 * 128
 MAIN = 28 * 128
-GROUP = 64
+GROUP = 50
 PACK = 2 * SLOTS * RUN_V
 ALL_VMEM = 64 * 1024 * 1024
 SOME_VMEM = 12 * 1024 * 1024
@@ -41,7 +41,7 @@
         for g in range(1, IRREPS):
             cand = low[g] + bit
             below = labels[jnp.minimum(cand, length) - 1] < g
-            low[g] = jnp.where((cand <= length) & below, cand, low[g])
+            low[g] = jnp.where(below, cand, low[g])
         bit //= 2
     for g in range(IRREPS):
         starts[g] = low[g]
@@ -205,9 +205,7 @@
         left[slot] = jnp.broadcast_to(column, (8, 128))
 
     lanes = lax.broadcasted_iota(jnp.int32, (RUN_O, 128), 1)
-    group[...] = jnp.zeros_like(group)
-
-    def symmetry(sym, carry):
+    for sym in range(IRREPS):
         turned = [[] for _ in range(ROWS_I)]
         for slot in range(SLOTS):
             g = vir_ref[c_first + slot] ^ sym
@@ -228,15 +226,16 @@
             for t, tile in enumerate(tiles_of(turned[i], lanes)):
                 if t == 7:
                     tile = jnp.where(lanes < HALF, tile, 0.0)
-                group[pl.ds(i * RUN_O, RUN_O), pl.ds(t * 128, 128)] = tile
-        tau = group[...]
-        top = tau.astype(jnp.bfloat16)
-        out = pl.ds(pl.multiple_of(sym * GROUP, GROUP), GROUP)
-        high[out, :] = top
-        low[out, :] = (tau - top.astype(jnp.float32)).astype(jnp.bfloat16)
-        return carry
-
-    lax.fori_loop(0, IRREPS, symmetry, 0)
+                group[pl.ds(sym * GROUP + i * RUN_O, RUN_O), pl.ds(t * 128, 128)] = tile
+    wide = group[:, pl.ds(0, FULL)]
+    top = wide.astype(jnp.bfloat16)
+    high[:, pl.ds(0, FULL)] = top
+    low[...] = (wide - top.astype(jnp.float32)).astype(jnp.bfloat16)
+    last = group[:, pl.ds(FULL, 128)]
+    upper = last.astype(jnp.bfloat16).astype(jnp.float32)
+    lanes_all = lax.broadcasted_iota(jnp.int32, last.shape, 1)
+    last = jnp.where(lanes_all < HALF, upper, pltpu.roll(last - upper, HALF, axis=1))
+    high[:, pl.ds(FULL, 128)] = last.astype(jnp.bfloat16)
 
 
 def spread_index(o, u, vir_ref, occ_ref, owner_ref, vlow, olow):
@@ -298,7 +297,7 @@
         out_specs=[vmem, vmem, vmem],
         out_shape=[
             jax.ShapeDtypeStruct((IRREPS * GROUP, depth), jnp.bfloat16),
-            jax.ShapeDtypeStruct((IRREPS * GROUP, depth), jnp.bfloat16),
+            jax.ShapeDtypeStruct((IRREPS * GROUP, FULL), jnp.bfloat16),
             jax.ShapeDtypeStruct((8, 256), jnp.int32),
         ],
         scratch_shapes=[
@@ -308,7 +307,7 @@
             pltpu.VMEM((5, NO + 16, 128), jnp.float32),
             pltpu.VMEM((IRREPS, 16, 128), jnp.float32),
             pltpu.VMEM((SLOTS, 8, 128), jnp.float32),
-            pltpu.VMEM((GROUP, depth), jnp.float32),
+            pltpu.VMEM((IRREPS * GROUP, depth), jnp.float32),
         ],
         compiler_params=pltpu.CompilerParams(vmem_limit_bytes=SOME_VMEM),
         cost_estimate=pl.CostEstimate(flops=0, bytes_accessed=8 * 1024 * 1024, transcendentals=0),
@@ -316,38 +315,47 @@
     )(vir_irrep, occ_irrep, owner, amplitudes, singles)
 
 
-def ladder_kernel(vir_ref, owner_ref, packed_ref, high, low, out_ref, vstart, top, bottom):
+def ladder_kernel(vir_ref, owner_ref, packed_ref, high, low, out_ref, vstart, top, bottom, sums):
     vlow = fill_starts(vir_ref, NV, vstart)
+    lanes = lax.broadcasted_iota(jnp.int32, (COLS, 128), 1)
     for source in range(8):
+        last = packed_ref[source, :, pl.ds(FULL, 128)]
+        other = pltpu.roll(last, HALF, axis=1)
         for s in range(2):
+            rows = pl.ds(s * SPAN + source * COLS, COLS)
             wide = packed_ref[source, :, pl.ds(s * (FULL + 128), FULL)]
-            last = packed_ref[source, :, pl.ds(FULL, 128)]
-            if s == 1:
-                last = pltpu.roll(last, HALF, axis=1)
-            rows = pl.ds(s * SPAN + source * COLS, COLS)
-            for part, at, size in ((wide, 0, FULL), (last, FULL, 128)):
-                upper = part.astype(jnp.bfloat16)
-                top[rows, pl.ds(at, size)] = upper
-                bottom[rows, pl.ds(at, size)] = (part - upper.astype(jnp.float32)).astype(jnp.bfloat16)
+            upper = wide.astype(jnp.bfloat16)
+            top[rows, pl.ds(0, FULL)] = upper
+            bottom[rows, pl.ds(0, FULL)] = (wide - upper.astype(jnp.float32)).astype(jnp.bfloat16)
+            twice = jnp.where(lanes < HALF, last, other) if s == 0 else jnp.where(lanes < HALF, other, last)
+            upper = twice.astype(jnp.bfloat16)
+            top[rows, pl.ds(FULL, 128)] = upper
+            rest = jnp.where(lanes < HALF, twice - upper.astype(jnp.float32), 0.0)
+            bottom[rows, pl.ds(FULL, 128)] = rest.astype(jnp.bfloat16)
     contract = functools.partial(
         lax.dot_general,
         dimension_numbers=(((1,), (1,)), ((), ())),
         preferred_element_type=jnp.float32,
     )
-    upper, lower = top[...], bottom[...]
-    sums = contract(upper, high[...]) + contract(lower, high[...]) + contract(upper, low[...])
-    column = lax.broadcasted_iota(jnp.int32, (2 * SPAN, 128), 0)
-    second = column >= NV
-    sym = irrep_of(jnp.where(second, column - NV, column), vlow)
-    sym = sym ^ jnp.where(second, vir_ref[1], vir_ref[0])
-    pair = sym >> 1
-    picked = sums[:, 0:128]
-    for t in range(1, 4):
-        picked = jnp.where(pair == t, sums[:, t * 128 : (t + 1) * 128], picked)
-    span = (column >= SPAN).astype(jnp.int32)
-    picked = jnp.where((sym & 1) == span, picked, pltpu.roll(picked, HALF, axis=1))
-    lanes = lax.broadcasted_iota(jnp.int32, (SPAN, 128), 1)
-    both = 0.5 * jnp.where(lanes < HALF, picked[:SPAN], picked[SPAN:])
+    used = IRREPS * GROUP
+    sums[pl.ds(0, used), :] = (
+        contract(high[...], top[...])
+        + contract(high[...], bottom[...])
+        + contract(low[...], top[:, pl.ds(0, FULL)])
+    )
+    sums[pl.ds(used, 8), :] = jnp.zeros((8, 2 * SPAN), jnp.float32)
+    halves = []
+    for s in range(2):
+        there = pl.ds(s * SPAN, SPAN)
+        column = lax.broadcasted_iota(jnp.int32, (56, SPAN), 1) + s * SPAN
+        second = column >= NV
+        sym = irrep_of(jnp.where(second, column - NV, column), vlow)
+        sym = sym ^ jnp.where(second, vir_ref[1], vir_ref[0])
+        picked = sums[pl.ds(0, 56), there]
+        for g in range(1, IRREPS):
+            picked = jnp.where(sym == g, sums[pl.ds(g * GROUP, 56), there], picked)
+        halves += [picked, jnp.zeros((HALF - 56, SPAN), jnp.float32)]
+    both = 0.5 * jnp.transpose(jnp.concatenate(halves, axis=0))
     for k in range(64):
         out_ref[owner_ref[k]] = both[4 * k : 4 * k + 4, :]
 
@@ -365,6 +373,7 @@
             pltpu.SMEM((IRREPS + 1,), jnp.int32),
             pltpu.VMEM((2 * SPAN, depth), jnp.bfloat16),
             pltpu.VMEM((2 * SPAN, depth), jnp.bfloat16),
+            pltpu.VMEM((IRREPS * GROUP + 8, 2 * SPAN), jnp.float32),
         ],
         compiler_params=pltpu.CompilerParams(vmem_limit_bytes=SOME_VMEM),
         name="ladder",

time: 76.6 us -> 74.9 us (0.978)
  local copies, waits for them, and re-layouts: 4.07 us -> 2.74 us
  Pallas kernels: 10.2 us -> 9.06 us
  waiting for transfers between devices: 17.8 us -> 18.6 us
    unnamed x14 -> x10, local copies, waits for them, and re-layouts: 4.07 us -> 2.74 us
    all_to_all x1, waiting for transfers between devices: 17.8 us -> 18.6 us  [shards(): gathered = lax.all_to_all(packed, 'occ', 0, 0, tiled=True)]
  transfers between devices with their start and end apart: 1 -> 1, of which waited for: 1 -> 1; matrix products, arithmetic and copies ran while one was open for 0% -> 0% of each run, Pallas kernels for 4% -> 3%
where the time goes in v4:
time: 74.9 us; the launch traced here: 74.6 us
  blocking collectives  38.1 us (51%)
  waiting for transfers between devices  18.6 us (25%)
  Pallas kernels  9.06 us (12%)
  starting transfers between devices  6.09 us (8%)
  local copies, waits for them, and re-layouts  2.74 us (4%)
    all_to_all x1, blocking collectives, shards(): parts = lax.all_to_all(mine, 'vir', 0, 0, tiled=True)  38.1 us
    all_to_all x1, waiting for transfers between devices, shards(): gathered = lax.all_to_all(packed, 'occ', 0, 0, tiled=True)  18.6 us
    all_to_all x1, starting transfers between devices, shards(): gathered = lax.all_to_all(packed, 'occ', 0, 0, tiled=True)  6.09 us
    pallas_call x1, Pallas kernels, pack(): pl.pallas_call(functools.partial(pack_kernel, where_am_i), in_specs=[anyw...  3.69 us
    unnamed x10, local copies, waits for them, and re-layouts  2.74 us
    pallas_call x1, Pallas kernels, tau(): pl.pallas_call(functools.partial(tau_kernel, where_am_i), in_specs=[smem,...  2.4 us
    pallas_call x1, Pallas kernels, ladder(): pl.pallas_call(ladder_kernel, in_specs=[smem, smem, vmem, vmem, vmem], ou...  2.22 us
  transfers between devices with their start and end apart: 1, of which 1 were waited for; matrix products, arithmetic and copies ran while one was open for 0% of the time, Pallas kernels for 3%

profile of v4, /device:TPU:1, one launch (start us, length us, event | category | flops | bytes accessed | tf_op | source)
XLA Modules:
  0.0 74.6 jit_solution(13078706510973666448)
XLA Ops:
  0.0 3.7 %pack.1 = f32[8,32,1920]{2,1,0:T(8,128)} custom-call(s32[480]{0:T(512)} %vir_ref.3, f32[2,32,3600]{2,1,0:T(8,128)} %bitcast.2), custom_call_target="tpu_custom_call" | custom-call | tf_op jit(solution)/shard_map/pack/pallas_call | solution.py:162
  3.7 0.0 copy-start.2
  3.7 0.0 copy-start.3
  3.7 0.0 copy-start.4
  3.7 6.1 %all-to-all-start = ((f32[8,32,1920]{2,1,0:T(8,128)}), f32[8,32,1920]{2,1,0:T(8,128)S(1)}, u32[]{:S(2)}, u32[]{:S(2)}) async-start(f32[8,32,1920]{2,1,0:T(8,128)} %pack.1), calls=%async_computation | async-start | bytes 3932160 | tf_op jit(solution)/shard_map/all_to_all | solution.py:408
  9.8 0.0 copy-done.2
  9.8 0.0 copy-done.3
  9.8 0.0 copy-done.4
  9.9 0.0 copy-start
  9.9 1.8 %copy-done = f32[200,3600]{1,0:T(8,128)S(1)} copy-done((f32[200,3600]{1,0:T(8,128)S(1)}, f32[200,3600]{1,0:T(8,128)}, u32[]{:S(2)}) %copy-start) | copy-done | bytes 2880024
  11.7 0.0 copy-start.1
  11.7 0.9 %copy-done.1 = f32[40,480]{1,0:T(8,128)S(1)} copy-done((f32[40,480]{1,0:T(8,128)S(1)}, f32[40,480]{1,0:T(8,128)}, u32[]{:S(2)}) %copy-start.1) | copy-done | bytes 76824
  12.6 2.4 %tau.1 = (bf16[400,1024]{1,0:T(8,128)(2,1)S(1)}, bf16[400,896]{1,0:T(8,128)(2,1)S(1)}, s32[8,256]{1,0:T(8,128)S(1)}) custom-call(s32[480]{0:T(512)S(1)} %copy-done.2, s32[40]{0:T(128)S(1)} %copy-done.4, s32[64]{0:T(128)S(1)} %copy-done.3, f32[200,3600]{1,0:T(8,128)S(1)} %copy-done, f32[40,480]{1,0:T(8,128)S(1)} %copy-done.1), custom_call_target="tpu_custom_call" | custom-call | bytes 8388608 | tf_op jit(solution)/shard_map/tau/pallas_call | solution.py:294
  15.0 18.6 %all-to-all-done.packed_ref = f32[8,32,1920]{2,1,0:T(8,128)S(1)} async-done(((f32[8,32,1920]{2,1,0:T(8,128)}), f32[8,32,1920]{2,1,0:T(8,128)S(1)}, u32[]{:S(2)}, u32[]{:S(2)}) %all-to-all-start) | async-done | bytes 1966112 | tf_op jit(solution)/shard_map/all_to_all | solution.py:408
  33.6 2.2 %ladder.1 = f32[64,4,128]{2,1,0:T(4,128)S(1)} custom-call(s32[480]{0:T(512)S(1)} %copy-done.2, s32[64]{0:T(128)S(1)} %copy-done.3, f32[8,32,1920]{2,1,0:T(8,128)S(1)} %all-to-all-done.packed_ref, bf16[400,1024]{1,0:T(8,128)(2,1)S(1)} %get-tuple-element.8.high, bf16[400,896]{1,0:T(8,128)(2,1)S(1)} %get-tuple-element.9.low), custom_call_target="tpu_custom_call" | custom-call | tf_op jit(solution)/shard_map/ladder/pallas_call | solution.py:367
  35.8 38.1 %all_to_all.10.parts_ref = f32[64,4,128]{2,1,0:T(4,128)S(1)} all-to-all(f32[64,4,128]{2,1,0:T(4,128)S(1)} %ladder.1), channel_id=1, replica_groups=mesh['occ'=8,'vir'=64] {'vir'}, dimensions={0} | all-to-all | bytes 262144 | tf_op jit(solution)/shard_map/all_to_all | solution.py:411
  73.9 0.7 finish.1
Async XLA Ops:
  3.7 6.1 %copy-start.2 = (s32[480]{0:T(512)S(1)}, s32[480]{0:T(512)}, u32[]{:S(2)}) copy-start(s32[480]{0:T(512)} %vir_ref.3) | copy-start | bytes 5764
  3.7 6.1 %copy-start.3 = (s32[64]{0:T(128)S(1)}, s32[64]{0:T(128)}, u32[]{:S(2)}) copy-start(s32[64]{0:T(128)} %owner_ref.3) | copy-start | bytes 772
  3.7 6.1 %copy-start.4 = (s32[40]{0:T(128)S(1)}, s32[40]{0:T(128)}, u32[]{:S(2)}) copy-start(s32[40]{0:T(128)} %occ_ref.1) | copy-start | bytes 484
  3.7 29.8 %all-to-all-start = ((f32[8,32,1920]{2,1,0:T(8,128)}), f32[8,32,1920]{2,1,0:T(8,128)S(1)}, u32[]{:S(2)}, u32[]{:S(2)}) async-start(f32[8,32,1920]{2,1,0:T(8,128)} %pack.1), calls=%async_computation | async-start | bytes 3932160 | tf_op jit(solution)/shard_map/all_to_all | solution.py:408
  9.9 1.8 %copy-start = (f32[200,3600]{1,0:T(8,128)S(1)}, f32[200,3600]{1,0:T(8,128)}, u32[]{:S(2)}) copy-start(f32[200,3600]{1,0:T(8,128)} %amp_ref.1) | copy-start | bytes 8640004
  11.7 0.9 %copy-start.1 = (f32[40,480]{1,0:T(8,128)S(1)}, f32[40,480]{1,0:T(8,128)}, u32[]{:S(2)}) copy-start(f32[40,480]{1,0:T(8,128)} %singles_ref.1) | copy-start | bytes 230404

commit v5 on v4

--- a/solution.py
+++ b/solution.py
@@ -57,8 +57,8 @@
 
 
 def turn(near, far, position, inner, lanes):
-    shift = lax.rem(position, 128)
-    amount = lax.rem(inner + 128 - shift, 128)
+    shift = position & 127
+    amount = (inner + 128 - shift) & 127
     return pltpu.roll(jnp.where(lanes >= shift, near, far), amount, axis=1)
 
 
@@ -73,7 +73,7 @@
 
 
 def first_pair(v):
-    return (v * 15) // 2, (v % 2) * (NV // 2)
+    return (v * 15) >> 1, (v & 1) * (NV // 2)
 
 
 def pack_kernel(where_am_i, vir_hbm, int_hbm, out_hbm, labels, starts, ints, whole, packed, sems):
@@ -83,11 +83,6 @@
     for s in range(2):
         copies.append(
             [
-                pltpu.make_async_copy(
-                    int_hbm.at[s, :, pl.ds(0, MAIN)],
-                    ints.at[s, :, pl.ds(LEAD, MAIN)],
-                    sems.at[1 + 2 * s],
-                ),
                 pltpu.make_async_copy(int_hbm.at[s], whole.at[s], sems.at[2 + 2 * s]),
             ]
         )
@@ -117,10 +112,12 @@
             sends.append(copy)
 
     held = None
+    irr_c = [labels[c_first + slot] for slot in range(SLOTS)]
+    begin = [LEAD - offset + low[g] for g in range(IRREPS)]
     for s in range(2):
         for copy in copies[s]:
             copy.wait()
-        ints[s, :, pl.ds(LEAD + MAIN, CD - MAIN)] = whole[s, :, pl.ds(MAIN, CD - MAIN)]
+        ints[s, :, pl.ds(LEAD, CD)] = whole[s]
         first = s * SPAN + o * COLS
         a = (first >= NV).astype(jnp.int32)
         b = first - a * NV
@@ -128,15 +125,16 @@
         irr_b = irrep_of(row + b, low)
         turned = []
         for slot in range(SLOTS):
-            cross = labels[c_first + slot] ^ irr_a
+            cross = irr_c[slot] ^ irr_a
+            mine = irr_b ^ cross
             value = jnp.zeros((COLS, 128), jnp.float32)
-            for h in range(IRREPS):
-                position = LEAD + slot * NV + starts[cross ^ h] - offset
-                base = pl.multiple_of((position // 128) * 128, 128)
+            for g in range(IRREPS):
+                position = begin[g] + slot * NV
+                base = pl.multiple_of(position & -128, 128)
                 near = ints[s, :, pl.ds(base, 128)]
                 far = ints[s, :, pl.ds(base + 128, 128)]
                 moved = turn(near, far, position, inner_of(slot), lanes)
-                value = jnp.where(irr_b == h, moved, value)
+                value = jnp.where(mine == g, moved, value)
             turned.append(value)
             at = s * (FULL + 128)
             if slot:
@@ -191,15 +189,15 @@
     lanes_w = lax.broadcasted_iota(jnp.int32, (16, 128), 1)
     for g in range(IRREPS):
         at, rows = vstart[g], pl.ds(ostart[g], 16)
-        single_win[g] = turn(ones[at // 128, rows, :], ones[at // 128 + 1, rows, :], at, 0, lanes_w)
+        single_win[g] = turn(ones[at >> 7, rows, :], ones[(at >> 7) + 1, rows, :], at, 0, lanes_w)
     lane_c = lax.broadcasted_iota(jnp.int32, (8, 128), 1)
     row_i = lax.broadcasted_iota(jnp.int32, (8, 1), 0)
     irr_i = [occ_ref[o * ROWS_I + i] for i in range(ROWS_I)]
     for slot in range(SLOTS):
         c = c_first + slot
         irr_c = vir_ref[c]
-        own = ones[c // 128, pl.ds(o * ROWS_I, 8), :]
-        column = jnp.sum(jnp.where(lane_c == lax.rem(c, 128), own, 0.0), axis=1, keepdims=True)
+        own = ones[c >> 7, pl.ds(o * ROWS_I, 8), :]
+        column = jnp.sum(jnp.where(lane_c == (c & 127), own, 0.0), axis=1, keepdims=True)
         for i in range(ROWS_I):
             column = jnp.where((row_i == i) & (irr_i[i] != irr_c), 0.0, column)
         left[slot] = jnp.broadcast_to(column, (8, 128))
@@ -215,7 +213,7 @@
             inner = inner_of(slot)
             k = (lanes + (128 - inner)) & 127
             keep = (k >= from_lane) & (k < to_lane)
-            near = (LEAD + begin) // 128
+            near = (LEAD + begin) >> 7
             right = pltpu.roll(single_win[g], inner, axis=1)[:RUN_O]
             for i in range(ROWS_I):
                 rows = pl.ds(i * NO + ostart[irr_i[i] ^ sym], RUN_O)
@@ -315,13 +313,24 @@
     )(vir_irrep, occ_irrep, owner, amplitudes, singles)
 
 
-def ladder_kernel(vir_ref, owner_ref, packed_ref, high, low, out_ref, vstart, top, bottom, sums):
+def ladder_kernel(
+    where_am_i, vir_ref, owner_ref, packed_ref, high, low, keep_ref, send_ref, vstart, top, bottom, sums, both_cores
+):
+    core = where_am_i()[1] & 1
     vlow = fill_starts(vir_ref, NV, vstart)
     lanes = lax.broadcasted_iota(jnp.int32, (COLS, 128), 1)
-    for source in range(8):
-        last = packed_ref[source, :, pl.ds(FULL, 128)]
-        other = pltpu.roll(last, HALF, axis=1)
-        for s in range(2):
+    contract = functools.partial(
+        lax.dot_general,
+        dimension_numbers=(((1,), (1,)), ((), ())),
+        preferred_element_type=jnp.float32,
+    )
+    used = IRREPS * GROUP
+    sums[pl.ds(used, 8), :] = jnp.zeros((8, 2 * SPAN), jnp.float32)
+
+    def split(s):
+        for source in range(8):
+            last = packed_ref[source, :, pl.ds(FULL, 128)]
+            other = pltpu.roll(last, HALF, axis=1)
             rows = pl.ds(s * SPAN + source * COLS, COLS)
             wide = packed_ref[source, :, pl.ds(s * (FULL + 128), FULL)]
             upper = wide.astype(jnp.bfloat16)
@@ -332,48 +341,54 @@
             top[rows, pl.ds(FULL, 128)] = upper
             rest = jnp.where(lanes < HALF, twice - upper.astype(jnp.float32), 0.0)
             bottom[rows, pl.ds(FULL, 128)] = rest.astype(jnp.bfloat16)
-    contract = functools.partial(
-        lax.dot_general,
-        dimension_numbers=(((1,), (1,)), ((), ())),
-        preferred_element_type=jnp.float32,
-    )
-    used = IRREPS * GROUP
-    sums[pl.ds(0, used), :] = (
-        contract(high[...], top[...])
-        + contract(high[...], bottom[...])
-        + contract(low[...], top[:, pl.ds(0, FULL)])
-    )
-    sums[pl.ds(used, 8), :] = jnp.zeros((8, 2 * SPAN), jnp.float32)
-    halves = []
-    for s in range(2):
+
+    def multiply(s):
         there = pl.ds(s * SPAN, SPAN)
-        column = lax.broadcasted_iota(jnp.int32, (56, SPAN), 1) + s * SPAN
+        sums[pl.ds(0, used), there] = (
+            contract(high[...], top[there, :])
+            + contract(high[...], bottom[there, :])
+            + contract(low[...], top[there, pl.ds(0, FULL)])
+        )
+
+    def pick(s):
+        there = pl.ds(s * SPAN, SPAN)
+        column = lax.broadcasted_iota(jnp.int32, (1, SPAN), 1) + s * SPAN
         second = column >= NV
         sym = irrep_of(jnp.where(second, column - NV, column), vlow)
         sym = sym ^ jnp.where(second, vir_ref[1], vir_ref[0])
         picked = sums[pl.ds(0, 56), there]
         for g in range(1, IRREPS):
             picked = jnp.where(sym == g, sums[pl.ds(g * GROUP, 56), there], picked)
-        halves += [picked, jnp.zeros((HALF - 56, SPAN), jnp.float32)]
-    both = 0.5 * jnp.transpose(jnp.concatenate(halves, axis=0))
+        return picked
+
+    split(0)
+    multiply(0)
+    split(1)
+    multiply(1)
+    pad = jnp.zeros((HALF - 56, SPAN), jnp.float32)
+    both = 0.5 * jnp.transpose(jnp.concatenate([pick(0), pad, pick(1), pad], axis=0))
     for k in range(64):
-        out_ref[owner_ref[k]] = both[4 * k : 4 * k + 4, :]
-
-
-def ladder(packed, high, low, vir_irrep, owner):
+        u = owner_ref[k]
+        both_cores[(u & 1) ^ core, u >> 1] = both[4 * k : 4 * k + 4, :]
+    keep_ref[...] = both_cores[0]
+    send_ref[...] = both_cores[1]
+
+
+def ladder(where_am_i, packed, high, low, vir_irrep, owner):
     smem = pl.BlockSpec(memory_space=pltpu.SMEM)
     vmem = pl.BlockSpec(memory_space=pltpu.VMEM)
     depth = SLOTS * 128
     return pl.pallas_call(
-        ladder_kernel,
+        functools.partial(ladder_kernel, where_am_i),
         in_specs=[smem, smem, vmem, vmem, vmem],
-        out_specs=vmem,
-        out_shape=jax.ShapeDtypeStruct((64, 4, 128), jnp.float32),
+        out_specs=[vmem, vmem],
+        out_shape=[jax.ShapeDtypeStruct((32, 4, 128), jnp.float32)] * 2,
         scratch_shapes=[
             pltpu.SMEM((IRREPS + 1,), jnp.int32),
             pltpu.VMEM((2 * SPAN, depth), jnp.bfloat16),
             pltpu.VMEM((2 * SPAN, depth), jnp.bfloat16),
             pltpu.VMEM((IRREPS * GROUP + 8, 2 * SPAN), jnp.float32),
+            pltpu.VMEM((2, 32, 4, 128), jnp.float32),
         ],
         compiler_params=pltpu.CompilerParams(vmem_limit_bytes=SOME_VMEM),
         name="ladder",
@@ -407,8 +422,10 @@
     packed = pack(placed, jnp.transpose(integrals, (0, 2, 1)), vir_irrep)
     gathered = lax.all_to_all(packed, "occ", 0, 0, tiled=True)
     high, low, index = tau(placed, amplitudes, singles, occ_irrep, vir_irrep, owner)
-    mine = ladder(gathered, high, low, vir_irrep, owner)
-    parts = lax.all_to_all(mine, "vir", 0, 0, tiled=True)
+    keep, send = ladder(placed, gathered, high, low, vir_irrep, owner)
+    keep += lax.ppermute(send, "vir", [(n, n ^ 1) for n in range(64)])
+    same_core = [list(range(core, 64, 2)) for core in range(2)]
+    parts = lax.all_to_all(keep, "vir", 0, 0, axis_index_groups=same_core, tiled=True)
     return jnp.transpose(finish(parts, index))
 
 

time: 74.9 us -> 72.2 us (0.964)
  blocking collectives: 38.1 us -> 31.2 us
  starting transfers between devices: 6.09 us -> 9.85 us
  waiting for transfers between devices: 18.6 us -> 19.6 us
  Pallas kernels: 9.06 us -> 8.31 us
    all_to_all x1, blocking collectives: 38.1 us -> 31.2 us  [shards(): lax.all_to_all(keep, 'vir', 0, 0, axis_index_groups=same_core, tiled=True)]
    ppermute x0 -> x1, starting transfers between devices: none -> 3.76 us  [shards(): keep += lax.ppermute(send, 'vir', [(n, n ^ 1) for n in range(64)])]
    ppermute x0 -> x1, waiting for transfers between devices: none -> 0.88 us  [shards(): keep += lax.ppermute(send, 'vir', [(n, n ^ 1) for n in range(64)])]
  transfers between devices with their start and end apart: 1 -> 2, of which waited for: 1 -> 2; matrix products, arithmetic and copies ran while one was open for 0% -> 0% of each run, Pallas kernels for 3% -> 3%
where the time goes in v5:
time: 72.2 us; the launch traced here: 71.9 us
  blocking collectives  31.2 us (43%)
  waiting for transfers between devices  19.6 us (27%)
  starting transfers between devices  9.85 us (14%)
  Pallas kernels  8.31 us (12%)
  local copies, waits for them, and re-layouts  2.74 us (4%)
    all_to_all x1, blocking collectives, shards(): lax.all_to_all(keep, 'vir', 0, 0, axis_index_groups=same_core, tiled=True)  31.2 us
    all_to_all x1, waiting for transfers between devices, shards(): gathered = lax.all_to_all(packed, 'occ', 0, 0, tiled=True)  18.8 us
    all_to_all x1, starting transfers between devices, shards(): gathered = lax.all_to_all(packed, 'occ', 0, 0, tiled=True)  6.09 us
    ppermute x1, starting transfers between devices, shards(): keep += lax.ppermute(send, 'vir', [(n, n ^ 1) for n in range(64)])  3.76 us
    pallas_call x1, Pallas kernels, pack(): pl.pallas_call(functools.partial(pack_kernel, where_am_i), in_specs=[anyw...  3.12 us
    unnamed x10, local copies, waits for them, and re-layouts  2.74 us
    pallas_call x1, Pallas kernels, ladder(): pl.pallas_call(functools.partial(ladder_kernel, where_am_i), in_specs=[sm...  2.27 us
    pallas_call x1, Pallas kernels, tau(): pl.pallas_call(functools.partial(tau_kernel, where_am_i), in_specs=[smem,...  2.22 us
  transfers between devices with their start and end apart: 2, of which 2 were waited for; matrix products, arithmetic and copies ran while one was open for 0% of the time, Pallas kernels for 3%

profile of v5, /device:TPU:1, one launch (start us, length us, event | category | flops | bytes accessed | tf_op | source)
XLA Modules:
  0.0 71.9 jit_solution(16131255397677290667)
XLA Ops:
  0.0 3.1 %pack.1 = f32[8,32,1920]{2,1,0:T(8,128)} custom-call(s32[480]{0:T(512)} %vir_ref.3, f32[2,32,3600]{2,1,0:T(8,128)} %bitcast.2), custom_call_target="tpu_custom_call" | custom-call | tf_op jit(solution)/shard_map/pack/pallas_call | solution.py:160
  3.1 0.0 copy-start.2
  3.1 0.0 copy-start.3
  3.2 0.0 copy-start.4
  3.2 6.1 %all-to-all-start = ((f32[8,32,1920]{2,1,0:T(8,128)}), f32[8,32,1920]{2,1,0:T(8,128)S(1)}, u32[]{:S(2)}, u32[]{:S(2)}) async-start(f32[8,32,1920]{2,1,0:T(8,128)} %pack.1), calls=%async_computation | async-start | bytes 3932160 | tf_op jit(solution)/shard_map/all_to_all | solution.py:423
  9.3 0.0 copy-done.2
  9.3 0.0 copy-done.3
  9.3 0.0 copy-done.4
  9.3 0.0 copy-start
  9.3 1.8 %copy-done = f32[200,3600]{1,0:T(8,128)S(1)} copy-done((f32[200,3600]{1,0:T(8,128)S(1)}, f32[200,3600]{1,0:T(8,128)}, u32[]{:S(2)}) %copy-start) | copy-done | bytes 2880024
  11.1 0.0 copy-start.1
  11.1 0.9 %copy-done.1 = f32[40,480]{1,0:T(8,128)S(1)} copy-done((f32[40,480]{1,0:T(8,128)S(1)}, f32[40,480]{1,0:T(8,128)}, u32[]{:S(2)}) %copy-start.1) | copy-done | bytes 76824
  12.0 2.2 %tau.1 = (bf16[400,1024]{1,0:T(8,128)(2,1)S(1)}, bf16[400,896]{1,0:T(8,128)(2,1)S(1)}, s32[8,256]{1,0:T(8,128)S(1)}) custom-call(s32[480]{0:T(512)S(1)} %copy-done.2, s32[40]{0:T(128)S(1)} %copy-done.4, s32[64]{0:T(128)S(1)} %copy-done.3, f32[200,3600]{1,0:T(8,128)S(1)} %copy-done, f32[40,480]{1,0:T(8,128)S(1)} %copy-done.1), custom_call_target="tpu_custom_call" | custom-call | bytes 8388608 | tf_op jit(solution)/shard_map/tau/pallas_call | solution.py:292
  14.2 18.8 %all-to-all-done.packed_ref = f32[8,32,1920]{2,1,0:T(8,128)S(1)} async-done(((f32[8,32,1920]{2,1,0:T(8,128)}), f32[8,32,1920]{2,1,0:T(8,128)S(1)}, u32[]{:S(2)}, u32[]{:S(2)}) %all-to-all-start) | async-done | bytes 1966112 | tf_op jit(solution)/shard_map/all_to_all | solution.py:423
  33.0 2.3 %ladder.1 = (f32[32,4,128]{2,1,0:T(4,128)S(1)}, f32[32,4,128]{2,1,0:T(4,128)S(1)}) custom-call(s32[480]{0:T(512)S(1)} %copy-done.2, s32[64]{0:T(128)S(1)} %copy-done.3, f32[8,32,1920]{2,1,0:T(8,128)S(1)} %all-to-all-done.packed_ref, bf16[400,1024]{1,0:T(8,128)(2,1)S(1)} %get-tuple-element.10.high, bf16[400,896]{1,0:T(8,128)(2,1)S(1)} %get-tuple-element.11.low), custom_call_target="tpu_custom_call" | custom-call | tf_op jit(solution)/shard_map/ladder/pallas_call | solution.py:381
  35.3 3.8 %collective-permute-start = (f32[32,4,128]{2,1,0:T(4,128)S(1)}, f32[32,4,128]{2,1,0:T(4,128)S(1)}, u32[]{:S(2)}, u32[]{:S(2)}) collective-permute-start(f32[32,4,128]{2,1,0:T(4,128)S(1)} %get-tuple-element.13), channel_id=1, source_target_pairs={{0,1},{1,0},{2,3},{3,2},{4,5},{5,4},{6,7},{7,6},{8,9},{9,8},{10,11... | collective-permute-start | bytes 196616 | tf_op jit(solution)/shard_map/ppermute | solution.py:426
  39.0 0.9 %collective-permute-done = f32[32,4,128]{2,1,0:T(4,128)S(1)} collective-permute-done((f32[32,4,128]{2,1,0:T(4,128)S(1)}, f32[32,4,128]{2,1,0:T(4,128)S(1)}, u32[]{:S(2)}, u32[]{:S(2)}) %collective-permute-start) | collective-permute-done | bytes 65568 | tf_op jit(solution)/shard_map/ppermute | solution.py:426
  39.9 31.2 %all_to_all.10.parts_ref = f32[32,4,128]{2,1,0:T(4,128)S(1)} all-to-all(f32[32,4,128]{2,1,0:T(4,128)S(1)} %add.3), channel_id=1, replica_groups={{0,2,4,6,8,10,12,14,16,18,20,22,24,26,28,30,32,34,36,38,40,42,44,46,48,..., dimensions={0} | all-to-all | bytes 131072 | tf_op jit(solution)/shard_map/all_to_all | solution.py:428
  71.2 0.7 finish.1
  (1 shorter events, 0.0 us)
Async XLA Ops:
  3.1 6.1 %copy-start.2 = (s32[480]{0:T(512)S(1)}, s32[480]{0:T(512)}, u32[]{:S(2)}) copy-start(s32[480]{0:T(512)} %vir_ref.3) | copy-start | bytes 5764
  3.1 6.1 %copy-start.3 = (s32[64]{0:T(128)S(1)}, s32[64]{0:T(128)}, u32[]{:S(2)}) copy-start(s32[64]{0:T(128)} %owner_ref.3) | copy-start | bytes 772
  3.2 6.1 %copy-start.4 = (s32[40]{0:T(128)S(1)}, s32[40]{0:T(128)}, u32[]{:S(2)}) copy-start(s32[40]{0:T(128)} %occ_ref.1) | copy-start | bytes 484
  3.2 29.8 %all-to-all-start = ((f32[8,32,1920]{2,1,0:T(8,128)}), f32[8,32,1920]{2,1,0:T(8,128)S(1)}, u32[]{:S(2)}, u32[]{:S(2)}) async-start(f32[8,32,1920]{2,1,0:T(8,128)} %pack.1), calls=%async_computation | async-start | bytes 3932160 | tf_op jit(solution)/shard_map/all_to_all | solution.py:423
  9.3 1.8 %copy-start = (f32[200,3600]{1,0:T(8,128)S(1)}, f32[200,3600]{1,0:T(8,128)}, u32[]{:S(2)}) copy-start(f32[200,3600]{1,0:T(8,128)} %amp_ref.1) | copy-start | bytes 8640004
  11.1 0.9 %copy-start.1 = (f32[40,480]{1,0:T(8,128)S(1)}, f32[40,480]{1,0:T(8,128)}, u32[]{:S(2)}) copy-start(f32[40,480]{1,0:T(8,128)} %singles_ref.1) | copy-start | bytes 230404
  35.3 4.7 %collective-permute-start = (f32[32,4,128]{2,1,0:T(4,128)S(1)}, f32[32,4,128]{2,1,0:T(4,128)S(1)}, u32[]{:S(2)}, u32[]{:S(2)}) collective-permute-start(f32[32,4,128]{2,1,0:T(4,128)S(1)} %get-tuple-element.13), channel_id=1, source_target_pairs={{0,1},{1,0},{2,3},{3,2},{4,5},{5,4},{6,7},{7,6},{8,9},{9,8},{10,11... | collective-permute-start | bytes 196616 | tf_op jit(solution)/shard_map/ppermute | solution.py:426

commit v6 on v5

--- a/solution.py
+++ b/solution.py
@@ -257,7 +257,8 @@
     for g in range(1, IRREPS):
         begin = jnp.where(irr_j == g, olow[g], begin)
     lane = i * RUN_O + j - begin + jnp.where(row >= 4, HALF, 0)
-    return jnp.where((sym ^ irr_i ^ irr_j) == 0, lane, -1)
+    wanted = ((sym ^ irr_i ^ irr_j) == 0) & (lanes < ROWS_I * NO)
+    return jnp.where(wanted, lane, -1)
 
 
 def tau_kernel(

time: 72.2 us -> 72.2 us (level)
  no operation moved by 1% of the time
where the time goes in v6:
time: 72.2 us; the launch traced here: 71.9 us
  blocking collectives  31.2 us (43%)
  waiting for transfers between devices  19.7 us (27%)
  starting transfers between devices  9.85 us (14%)
  Pallas kernels  8.3 us (11%)
  local copies, waits for them, and re-layouts  2.74 us (4%)
    all_to_all x1, blocking collectives, shards(): lax.all_to_all(keep, 'vir', 0, 0, axis_index_groups=same_core, tiled=True)  31.2 us
    all_to_all x1, waiting for transfers between devices, shards(): gathered = lax.all_to_all(packed, 'occ', 0, 0, tiled=True)  18.8 us
    all_to_all x1, starting transfers between devices, shards(): gathered = lax.all_to_all(packed, 'occ', 0, 0, tiled=True)  6.09 us
    ppermute x1, starting transfers between devices, shards(): keep += lax.ppermute(send, 'vir', [(n, n ^ 1) for n in range(64)])  3.76 us
    pallas_call x1, Pallas kernels, pack(): pl.pallas_call(functools.partial(pack_kernel, where_am_i), in_specs=[anyw...  3.12 us
    unnamed x10, local copies, waits for them, and re-layouts  2.74 us
    pallas_call x1, Pallas kernels, ladder(): pl.pallas_call(functools.partial(ladder_kernel, where_am_i), in_specs=[sm...  2.27 us
    pallas_call x1, Pallas kernels, tau(): pl.pallas_call(functools.partial(tau_kernel, where_am_i), in_specs=[smem,...  2.2 us
  transfers between devices with their start and end apart: 2, of which 2 were waited for; matrix products, arithmetic and copies ran while one was open for 0% of the time, Pallas kernels for 3%

profile of v6, /device:TPU:1, one launch (start us, length us, event | category | flops | bytes accessed | tf_op | source)
XLA Modules:
  0.0 71.9 jit_solution(7982733899829441609)
XLA Ops:
  0.0 3.1 %pack.1 = f32[8,32,1920]{2,1,0:T(8,128)} custom-call(s32[480]{0:T(512)} %vir_ref.3, f32[2,32,3600]{2,1,0:T(8,128)} %bitcast.2), custom_call_target="tpu_custom_call" | custom-call | tf_op jit(solution)/shard_map/pack/pallas_call | solution.py:160
  3.1 0.0 copy-start.2
  3.1 0.0 copy-start.3
  3.2 0.0 copy-start.4
  3.2 6.1 %all-to-all-start = ((f32[8,32,1920]{2,1,0:T(8,128)}), f32[8,32,1920]{2,1,0:T(8,128)S(1)}, u32[]{:S(2)}, u32[]{:S(2)}) async-start(f32[8,32,1920]{2,1,0:T(8,128)} %pack.1), calls=%async_computation | async-start | bytes 3932160 | tf_op jit(solution)/shard_map/all_to_all | solution.py:424
  9.3 0.0 copy-done.2
  9.3 0.0 copy-done.3
  9.3 0.0 copy-done.4
  9.3 0.0 copy-start
  9.3 1.8 %copy-done = f32[200,3600]{1,0:T(8,128)S(1)} copy-done((f32[200,3600]{1,0:T(8,128)S(1)}, f32[200,3600]{1,0:T(8,128)}, u32[]{:S(2)}) %copy-start) | copy-done | bytes 2880024
  11.1 0.0 copy-start.1
  11.1 0.9 %copy-done.1 = f32[40,480]{1,0:T(8,128)S(1)} copy-done((f32[40,480]{1,0:T(8,128)S(1)}, f32[40,480]{1,0:T(8,128)}, u32[]{:S(2)}) %copy-start.1) | copy-done | bytes 76824
  12.0 2.2 %tau.1 = (bf16[400,1024]{1,0:T(8,128)(2,1)S(1)}, bf16[400,896]{1,0:T(8,128)(2,1)S(1)}, s32[8,256]{1,0:T(8,128)S(1)}) custom-call(s32[480]{0:T(512)S(1)} %copy-done.2, s32[40]{0:T(128)S(1)} %copy-done.4, s32[64]{0:T(128)S(1)} %copy-done.3, f32[200,3600]{1,0:T(8,128)S(1)} %copy-done, f32[40,480]{1,0:T(8,128)S(1)} %copy-done.1), custom_call_target="tpu_custom_call" | custom-call | bytes 8388608 | tf_op jit(solution)/shard_map/tau/pallas_call | solution.py:293
  14.2 18.8 %all-to-all-done.packed_ref = f32[8,32,1920]{2,1,0:T(8,128)S(1)} async-done(((f32[8,32,1920]{2,1,0:T(8,128)}), f32[8,32,1920]{2,1,0:T(8,128)S(1)}, u32[]{:S(2)}, u32[]{:S(2)}) %all-to-all-start) | async-done | bytes 1966112 | tf_op jit(solution)/shard_map/all_to_all | solution.py:424
  33.0 2.3 %ladder.1 = (f32[32,4,128]{2,1,0:T(4,128)S(1)}, f32[32,4,128]{2,1,0:T(4,128)S(1)}) custom-call(s32[480]{0:T(512)S(1)} %copy-done.2, s32[64]{0:T(128)S(1)} %copy-done.3, f32[8,32,1920]{2,1,0:T(8,128)S(1)} %all-to-all-done.packed_ref, bf16[400,1024]{1,0:T(8,128)(2,1)S(1)} %get-tuple-element.10.high, bf16[400,896]{1,0:T(8,128)(2,1)S(1)} %get-tuple-element.11.low), custom_call_target="tpu_custom_call" | custom-call | tf_op jit(solution)/shard_map/ladder/pallas_call | solution.py:382
  35.3 3.8 %collective-permute-start = (f32[32,4,128]{2,1,0:T(4,128)S(1)}, f32[32,4,128]{2,1,0:T(4,128)S(1)}, u32[]{:S(2)}, u32[]{:S(2)}) collective-permute-start(f32[32,4,128]{2,1,0:T(4,128)S(1)} %get-tuple-element.13), channel_id=1, source_target_pairs={{0,1},{1,0},{2,3},{3,2},{4,5},{5,4},{6,7},{7,6},{8,9},{9,8},{10,11... | collective-permute-start | bytes 196616 | tf_op jit(solution)/shard_map/ppermute | solution.py:427
  39.0 0.9 %collective-permute-done = f32[32,4,128]{2,1,0:T(4,128)S(1)} collective-permute-done((f32[32,4,128]{2,1,0:T(4,128)S(1)}, f32[32,4,128]{2,1,0:T(4,128)S(1)}, u32[]{:S(2)}, u32[]{:S(2)}) %collective-permute-start) | collective-permute-done | bytes 65568 | tf_op jit(solution)/shard_map/ppermute | solution.py:427
  39.9 31.2 %all_to_all.10.parts_ref = f32[32,4,128]{2,1,0:T(4,128)S(1)} all-to-all(f32[32,4,128]{2,1,0:T(4,128)S(1)} %add.3), channel_id=1, replica_groups={{0,2,4,6,8,10,12,14,16,18,20,22,24,26,28,30,32,34,36,38,40,42,44,46,48,..., dimensions={0} | all-to-all | bytes 131072 | tf_op jit(solution)/shard_map/all_to_all | solution.py:429
  71.2 0.7 finish.1
  (1 shorter events, 0.0 us)
Async XLA Ops:
  3.1 6.1 %copy-start.2 = (s32[480]{0:T(512)S(1)}, s32[480]{0:T(512)}, u32[]{:S(2)}) copy-start(s32[480]{0:T(512)} %vir_ref.3) | copy-start | bytes 5764
  3.1 6.1 %copy-start.3 = (s32[64]{0:T(128)S(1)}, s32[64]{0:T(128)}, u32[]{:S(2)}) copy-start(s32[64]{0:T(128)} %owner_ref.3) | copy-start | bytes 772
  3.2 6.1 %copy-start.4 = (s32[40]{0:T(128)S(1)}, s32[40]{0:T(128)}, u32[]{:S(2)}) copy-start(s32[40]{0:T(128)} %occ_ref.1) | copy-start | bytes 484
  3.2 29.8 %all-to-all-start = ((f32[8,32,1920]{2,1,0:T(8,128)}), f32[8,32,1920]{2,1,0:T(8,128)S(1)}, u32[]{:S(2)}, u32[]{:S(2)}) async-start(f32[8,32,1920]{2,1,0:T(8,128)} %pack.1), calls=%async_computation | async-start | bytes 3932160 | tf_op jit(solution)/shard_map/all_to_all | solution.py:424
  9.3 1.8 %copy-start = (f32[200,3600]{1,0:T(8,128)S(1)}, f32[200,3600]{1,0:T(8,128)}, u32[]{:S(2)}) copy-start(f32[200,3600]{1,0:T(8,128)} %amp_ref.1) | copy-start | bytes 8640004
  11.1 0.9 %copy-start.1 = (f32[40,480]{1,0:T(8,128)S(1)}, f32[40,480]{1,0:T(8,128)}, u32[]{:S(2)}) copy-start(f32[40,480]{1,0:T(8,128)} %singles_ref.1) | copy-start | bytes 230404
  35.3 4.7 %collective-permute-start = (f32[32,4,128]{2,1,0:T(4,128)S(1)}, f32[32,4,128]{2,1,0:T(4,128)S(1)}, u32[]{:S(2)}, u32[]{:S(2)}) collective-permute-start(f32[32,4,128]{2,1,0:T(4,128)S(1)} %get-tuple-element.13), channel_id=1, source_target_pairs={{0,1},{1,0},{2,3},{3,2},{4,5},{5,4},{6,7},{7,6},{8,9},{9,8},{10,11... | collective-permute-start | bytes 196616 | tf_op jit(solution)/shard_map/ppermute | solution.py:427

commit v7 on v6

--- a/solution.py
+++ b/solution.py
@@ -314,6 +314,11 @@
     )(vir_irrep, occ_irrep, owner, amplitudes, singles)
 
 
+def place_of(u):
+    z = u >> 2
+    return ((z & 7) << 2) | ((z >> 3) << 1) | ((u >> 1) & 1)
+
+
 def ladder_kernel(
     where_am_i, vir_ref, owner_ref, packed_ref, high, low, keep_ref, send_ref, vstart, top, bottom, sums, both_cores
 ):
@@ -370,7 +375,7 @@
     both = 0.5 * jnp.transpose(jnp.concatenate([pick(0), pad, pick(1), pad], axis=0))
     for k in range(64):
         u = owner_ref[k]
-        both_cores[(u & 1) ^ core, u >> 1] = both[4 * k : 4 * k + 4, :]
+        both_cores[(u & 1) ^ core, place_of(u)] = both[4 * k : 4 * k + 4, :]
     keep_ref[...] = both_cores[0]
     send_ref[...] = both_cores[1]
 
@@ -425,7 +430,7 @@
     high, low, index = tau(placed, amplitudes, singles, occ_irrep, vir_irrep, owner)
     keep, send = ladder(placed, gathered, high, low, vir_irrep, owner)
     keep += lax.ppermute(send, "vir", [(n, n ^ 1) for n in range(64)])
-    same_core = [list(range(core, 64, 2)) for core in range(2)]
+    same_core = [sorted(range(core, 64, 2), key=place_of) for core in range(2)]
     parts = lax.all_to_all(keep, "vir", 0, 0, axis_index_groups=same_core, tiled=True)
     return jnp.transpose(finish(parts, index))
 

time: 72.2 us -> 71.7 us (level)
  no operation moved by 1% of the time
where the time goes in v7:
time: 71.7 us; the launch traced here: 71.4 us
  blocking collectives  30.6 us (43%)
  waiting for transfers between devices  19.6 us (27%)
  starting transfers between devices  9.85 us (14%)
  Pallas kernels  8.44 us (12%)
  local copies, waits for them, and re-layouts  2.74 us (4%)
    all_to_all x1, blocking collectives, shards(): lax.all_to_all(keep, 'vir', 0, 0, axis_index_groups=same_core, tiled=True)  30.6 us
    all_to_all x1, waiting for transfers between devices, shards(): gathered = lax.all_to_all(packed, 'occ', 0, 0, tiled=True)  18.8 us
    all_to_all x1, starting transfers between devices, shards(): gathered = lax.all_to_all(packed, 'occ', 0, 0, tiled=True)  6.09 us
    ppermute x1, starting transfers between devices, shards(): keep += lax.ppermute(send, 'vir', [(n, n ^ 1) for n in range(64)])  3.76 us
    pallas_call x1, Pallas kernels, pack(): pl.pallas_call(functools.partial(pack_kernel, where_am_i), in_specs=[anyw...  3.13 us
    unnamed x10, local copies, waits for them, and re-layouts  2.74 us
    pallas_call x1, Pallas kernels, ladder(): pl.pallas_call(functools.partial(ladder_kernel, where_am_i), in_specs=[sm...  2.39 us
    pallas_call x1, Pallas kernels, tau(): pl.pallas_call(functools.partial(tau_kernel, where_am_i), in_specs=[smem,...  2.22 us
  transfers between devices with their start and end apart: 2, of which 2 were waited for; matrix products, arithmetic and copies ran while one was open for 0% of the time, Pallas kernels for 3%

profile of v7, /device:TPU:1, one launch (start us, length us, event | category | flops | bytes accessed | tf_op | source)
XLA Modules:
  0.0 71.4 jit_solution(274810102287688539)
XLA Ops:
  0.0 3.1 %pack.1 = f32[8,32,1920]{2,1,0:T(8,128)} custom-call(s32[480]{0:T(512)} %vir_ref.3, f32[2,32,3600]{2,1,0:T(8,128)} %bitcast.2), custom_call_target="tpu_custom_call" | custom-call | tf_op jit(solution)/shard_map/pack/pallas_call | solution.py:160
  3.1 0.0 copy-start.2
  3.1 0.0 copy-start.3
  3.2 0.0 copy-start.4
  3.2 6.1 %all-to-all-start = ((f32[8,32,1920]{2,1,0:T(8,128)}), f32[8,32,1920]{2,1,0:T(8,128)S(1)}, u32[]{:S(2)}, u32[]{:S(2)}) async-start(f32[8,32,1920]{2,1,0:T(8,128)} %pack.1), calls=%async_computation | async-start | bytes 3932160 | tf_op jit(solution)/shard_map/all_to_all | solution.py:429
  9.3 0.0 copy-done.2
  9.3 0.0 copy-done.3
  9.3 0.0 copy-done.4
  9.3 0.0 copy-start
  9.3 1.8 %copy-done = f32[200,3600]{1,0:T(8,128)S(1)} copy-done((f32[200,3600]{1,0:T(8,128)S(1)}, f32[200,3600]{1,0:T(8,128)}, u32[]{:S(2)}) %copy-start) | copy-done | bytes 2880024
  11.1 0.0 copy-start.1
  11.1 0.9 %copy-done.1 = f32[40,480]{1,0:T(8,128)S(1)} copy-done((f32[40,480]{1,0:T(8,128)S(1)}, f32[40,480]{1,0:T(8,128)}, u32[]{:S(2)}) %copy-start.1) | copy-done | bytes 76824
  12.0 2.2 %tau.1 = (bf16[400,1024]{1,0:T(8,128)(2,1)S(1)}, bf16[400,896]{1,0:T(8,128)(2,1)S(1)}, s32[8,256]{1,0:T(8,128)S(1)}) custom-call(s32[480]{0:T(512)S(1)} %copy-done.2, s32[40]{0:T(128)S(1)} %copy-done.4, s32[64]{0:T(128)S(1)} %copy-done.3, f32[200,3600]{1,0:T(8,128)S(1)} %copy-done, f32[40,480]{1,0:T(8,128)S(1)} %copy-done.1), custom_call_target="tpu_custom_call" | custom-call | bytes 8388608 | tf_op jit(solution)/shard_map/tau/pallas_call | solution.py:293
  14.2 18.8 %all-to-all-done.packed_ref = f32[8,32,1920]{2,1,0:T(8,128)S(1)} async-done(((f32[8,32,1920]{2,1,0:T(8,128)}), f32[8,32,1920]{2,1,0:T(8,128)S(1)}, u32[]{:S(2)}, u32[]{:S(2)}) %all-to-all-start) | async-done | bytes 1966112 | tf_op jit(solution)/shard_map/all_to_all | solution.py:429
  33.0 2.4 %ladder.1 = (f32[32,4,128]{2,1,0:T(4,128)S(1)}, f32[32,4,128]{2,1,0:T(4,128)S(1)}) custom-call(s32[480]{0:T(512)S(1)} %copy-done.2, s32[64]{0:T(128)S(1)} %copy-done.3, f32[8,32,1920]{2,1,0:T(8,128)S(1)} %all-to-all-done.packed_ref, bf16[400,1024]{1,0:T(8,128)(2,1)S(1)} %get-tuple-element.10.high, bf16[400,896]{1,0:T(8,128)(2,1)S(1)} %get-tuple-element.11.low), custom_call_target="tpu_custom_call" | custom-call | tf_op jit(solution)/shard_map/ladder/pallas_call | solution.py:387
  35.4 3.8 %collective-permute-start = (f32[32,4,128]{2,1,0:T(4,128)S(1)}, f32[32,4,128]{2,1,0:T(4,128)S(1)}, u32[]{:S(2)}, u32[]{:S(2)}) collective-permute-start(f32[32,4,128]{2,1,0:T(4,128)S(1)} %get-tuple-element.13), channel_id=1, source_target_pairs={{0,1},{1,0},{2,3},{3,2},{4,5},{5,4},{6,7},{7,6},{8,9},{9,8},{10,11... | collective-permute-start | bytes 196616 | tf_op jit(solution)/shard_map/ppermute | solution.py:432
  39.2 0.9 %collective-permute-done = f32[32,4,128]{2,1,0:T(4,128)S(1)} collective-permute-done((f32[32,4,128]{2,1,0:T(4,128)S(1)}, f32[32,4,128]{2,1,0:T(4,128)S(1)}, u32[]{:S(2)}, u32[]{:S(2)}) %collective-permute-start) | collective-permute-done | bytes 65568 | tf_op jit(solution)/shard_map/ppermute | solution.py:432
  40.1 30.6 %all_to_all.10.parts_ref = f32[32,4,128]{2,1,0:T(4,128)S(1)} all-to-all(f32[32,4,128]{2,1,0:T(4,128)S(1)} %add.3), channel_id=1, replica_groups={{0,2,32,34,4,6,36,38,8,10,40,42,12,14,44,46,16,18,48,50,20,22,52,54,24,..., dimensions={0} | all-to-all | bytes 131072 | tf_op jit(solution)/shard_map/all_to_all | solution.py:434
  70.7 0.7 finish.1
  (1 shorter events, 0.0 us)
Async XLA Ops:
  3.1 6.1 %copy-start.2 = (s32[480]{0:T(512)S(1)}, s32[480]{0:T(512)}, u32[]{:S(2)}) copy-start(s32[480]{0:T(512)} %vir_ref.3) | copy-start | bytes 5764
  3.1 6.1 %copy-start.3 = (s32[64]{0:T(128)S(1)}, s32[64]{0:T(128)}, u32[]{:S(2)}) copy-start(s32[64]{0:T(128)} %owner_ref.3) | copy-start | bytes 772
  3.2 6.1 %copy-start.4 = (s32[40]{0:T(128)S(1)}, s32[40]{0:T(128)}, u32[]{:S(2)}) copy-start(s32[40]{0:T(128)} %occ_ref.1) | copy-start | bytes 484
  3.2 29.8 %all-to-all-start = ((f32[8,32,1920]{2,1,0:T(8,128)}), f32[8,32,1920]{2,1,0:T(8,128)S(1)}, u32[]{:S(2)}, u32[]{:S(2)}) async-start(f32[8,32,1920]{2,1,0:T(8,128)} %pack.1), calls=%async_computation | async-start | bytes 3932160 | tf_op jit(solution)/shard_map/all_to_all | solution.py:429
  9.3 1.8 %copy-start = (f32[200,3600]{1,0:T(8,128)S(1)}, f32[200,3600]{1,0:T(8,128)}, u32[]{:S(2)}) copy-start(f32[200,3600]{1,0:T(8,128)} %amp_ref.1) | copy-start | bytes 8640004
  11.1 0.9 %copy-start.1 = (f32[40,480]{1,0:T(8,128)S(1)}, f32[40,480]{1,0:T(8,128)}, u32[]{:S(2)}) copy-start(f32[40,480]{1,0:T(8,128)} %singles_ref.1) | copy-start | bytes 230404
  35.4 4.6 %collective-permute-start = (f32[32,4,128]{2,1,0:T(4,128)S(1)}, f32[32,4,128]{2,1,0:T(4,128)S(1)}, u32[]{:S(2)}, u32[]{:S(2)}) collective-permute-start(f32[32,4,128]{2,1,0:T(4,128)S(1)} %get-tuple-element.13), channel_id=1, source_target_pairs={{0,1},{1,0},{2,3},{3,2},{4,5},{5,4},{6,7},{7,6},{8,9},{9,8},{10,11... | collective-permute-start | bytes 196616 | tf_op jit(solution)/shard_map/ppermute | solution.py:432

commit v8 on v7

--- a/solution.py
+++ b/solution.py
@@ -26,6 +26,8 @@
 SOME_VMEM = 12 * 1024 * 1024
 FULL = 7 * 128
 HALF = 64
+
+OCC_ORDER = (0, 5, 2, 7, 4, 1, 6, 3)
 
 
 def placed():
@@ -337,7 +339,7 @@
         for source in range(8):
             last = packed_ref[source, :, pl.ds(FULL, 128)]
             other = pltpu.roll(last, HALF, axis=1)
-            rows = pl.ds(s * SPAN + source * COLS, COLS)
+            rows = pl.ds(s * SPAN + OCC_ORDER[source] * COLS, COLS)
             wide = packed_ref[source, :, pl.ds(s * (FULL + 128), FULL)]
             upper = wide.astype(jnp.bfloat16)
             top[rows, pl.ds(0, FULL)] = upper
@@ -426,7 +428,9 @@
 
 def shards(amplitudes, singles, integrals, occ_irrep, vir_irrep, owner):
     packed = pack(placed, jnp.transpose(integrals, (0, 2, 1)), vir_irrep)
-    gathered = lax.all_to_all(packed, "occ", 0, 0, tiled=True)
+    gathered = lax.all_to_all(
+        packed, "occ", 0, 0, axis_index_groups=[list(OCC_ORDER)], tiled=True
+    )
     high, low, index = tau(placed, amplitudes, singles, occ_irrep, vir_irrep, owner)
     keep, send = ladder(placed, gathered, high, low, vir_irrep, owner)
     keep += lax.ppermute(send, "vir", [(n, n ^ 1) for n in range(64)])

time: 71.7 us -> 71.7 us (level)
  no operation moved by 1% of the time
where the time goes in v8:
time: 71.7 us; the launch traced here: 71.4 us
  blocking collectives  30.6 us (43%)
  waiting for transfers between devices  19.7 us (27%)
  starting transfers between devices  9.84 us (14%)
  Pallas kernels  8.44 us (12%)
  local copies, waits for them, and re-layouts  2.74 us (4%)
    all_to_all x1, blocking collectives, shards(): lax.all_to_all(keep, 'vir', 0, 0, axis_index_groups=same_core, tiled=True)  30.6 us
    all_to_all x1, waiting for transfers between devices, shards(): lax.all_to_all(packed, 'occ', 0, 0, axis_index_groups=[list(OCC_ORDER)],...  18.8 us
    all_to_all x1, starting transfers between devices, shards(): lax.all_to_all(packed, 'occ', 0, 0, axis_index_groups=[list(OCC_ORDER)],...  6.09 us
    ppermute x1, starting transfers between devices, shards(): keep += lax.ppermute(send, 'vir', [(n, n ^ 1) for n in range(64)])  3.75 us
    pallas_call x1, Pallas kernels, pack(): pl.pallas_call(functools.partial(pack_kernel, where_am_i), in_specs=[anyw...  3.12 us
    unnamed x10, local copies, waits for them, and re-layouts  2.74 us
    pallas_call x1, Pallas kernels, ladder(): pl.pallas_call(functools.partial(ladder_kernel, where_am_i), in_specs=[sm...  2.4 us
    pallas_call x1, Pallas kernels, tau(): pl.pallas_call(functools.partial(tau_kernel, where_am_i), in_specs=[smem,...  2.21 us
  transfers between devices with their start and end apart: 2, of which 2 were waited for; matrix products, arithmetic and copies ran while one was open for 0% of the time, Pallas kernels for 3%

profile of v8, /device:TPU:1, one launch (start us, length us, event | category | flops | bytes accessed | tf_op | source)
XLA Modules:
  0.0 71.4 jit_solution(10856152703239067993)
XLA Ops:
  0.0 3.1 %pack.1 = f32[8,32,1920]{2,1,0:T(8,128)} custom-call(s32[480]{0:T(512)} %vir_ref.3, f32[2,32,3600]{2,1,0:T(8,128)} %bitcast.2), custom_call_target="tpu_custom_call" | custom-call | tf_op jit(solution)/shard_map/pack/pallas_call | solution.py:162
  3.1 0.0 copy-start.2
  3.1 0.0 copy-start.3
  3.2 0.0 copy-start.4
  3.2 6.1 %all-to-all-start = ((f32[8,32,1920]{2,1,0:T(8,128)}), f32[8,32,1920]{2,1,0:T(8,128)S(1)}, u32[]{:S(2)}, u32[]{:S(2)}) async-start(f32[8,32,1920]{2,1,0:T(8,128)} %pack.1), calls=%async_computation | async-start | bytes 3932160 | tf_op jit(solution)/shard_map/all_to_all | solution.py:431
  9.3 0.0 copy-done.2
  9.3 0.0 copy-done.3
  9.3 0.0 copy-done.4
  9.3 0.0 copy-start
  9.3 1.8 %copy-done = f32[200,3600]{1,0:T(8,128)S(1)} copy-done((f32[200,3600]{1,0:T(8,128)S(1)}, f32[200,3600]{1,0:T(8,128)}, u32[]{:S(2)}) %copy-start) | copy-done | bytes 2880024
  11.1 0.0 copy-start.1
  11.1 0.9 %copy-done.1 = f32[40,480]{1,0:T(8,128)S(1)} copy-done((f32[40,480]{1,0:T(8,128)S(1)}, f32[40,480]{1,0:T(8,128)}, u32[]{:S(2)}) %copy-start.1) | copy-done | bytes 76824
  12.0 2.2 %tau.1 = (bf16[400,1024]{1,0:T(8,128)(2,1)S(1)}, bf16[400,896]{1,0:T(8,128)(2,1)S(1)}, s32[8,256]{1,0:T(8,128)S(1)}) custom-call(s32[480]{0:T(512)S(1)} %copy-done.2, s32[40]{0:T(128)S(1)} %copy-done.4, s32[64]{0:T(128)S(1)} %copy-done.3, f32[200,3600]{1,0:T(8,128)S(1)} %copy-done, f32[40,480]{1,0:T(8,128)S(1)} %copy-done.1), custom_call_target="tpu_custom_call" | custom-call | bytes 8388608 | tf_op jit(solution)/shard_map/tau/pallas_call | solution.py:295
  14.2 18.8 %all-to-all-done.packed_ref = f32[8,32,1920]{2,1,0:T(8,128)S(1)} async-done(((f32[8,32,1920]{2,1,0:T(8,128)}), f32[8,32,1920]{2,1,0:T(8,128)S(1)}, u32[]{:S(2)}, u32[]{:S(2)}) %all-to-all-start) | async-done | bytes 1966112 | tf_op jit(solution)/shard_map/all_to_all | solution.py:431
  33.0 2.4 %ladder.1 = (f32[32,4,128]{2,1,0:T(4,128)S(1)}, f32[32,4,128]{2,1,0:T(4,128)S(1)}) custom-call(s32[480]{0:T(512)S(1)} %copy-done.2, s32[64]{0:T(128)S(1)} %copy-done.3, f32[8,32,1920]{2,1,0:T(8,128)S(1)} %all-to-all-done.packed_ref, bf16[400,1024]{1,0:T(8,128)(2,1)S(1)} %get-tuple-element.10.high, bf16[400,896]{1,0:T(8,128)(2,1)S(1)} %get-tuple-element.11.low), custom_call_target="tpu_custom_call" | custom-call | tf_op jit(solution)/shard_map/ladder/pallas_call | solution.py:389
  35.4 3.8 %collective-permute-start = (f32[32,4,128]{2,1,0:T(4,128)S(1)}, f32[32,4,128]{2,1,0:T(4,128)S(1)}, u32[]{:S(2)}, u32[]{:S(2)}) collective-permute-start(f32[32,4,128]{2,1,0:T(4,128)S(1)} %get-tuple-element.13), channel_id=1, source_target_pairs={{0,1},{1,0},{2,3},{3,2},{4,5},{5,4},{6,7},{7,6},{8,9},{9,8},{10,11... | collective-permute-start | bytes 196616 | tf_op jit(solution)/shard_map/ppermute | solution.py:436
  39.2 0.9 %collective-permute-done = f32[32,4,128]{2,1,0:T(4,128)S(1)} collective-permute-done((f32[32,4,128]{2,1,0:T(4,128)S(1)}, f32[32,4,128]{2,1,0:T(4,128)S(1)}, u32[]{:S(2)}, u32[]{:S(2)}) %collective-permute-start) | collective-permute-done | bytes 65568 | tf_op jit(solution)/shard_map/ppermute | solution.py:436
  40.1 30.6 %all_to_all.10.parts_ref = f32[32,4,128]{2,1,0:T(4,128)S(1)} all-to-all(f32[32,4,128]{2,1,0:T(4,128)S(1)} %add.3), channel_id=1, replica_groups={{0,2,32,34,4,6,36,38,8,10,40,42,12,14,44,46,16,18,48,50,20,22,52,54,24,..., dimensions={0} | all-to-all | bytes 131072 | tf_op jit(solution)/shard_map/all_to_all | solution.py:438
  70.7 0.7 finish.1
  (1 shorter events, 0.0 us)
Async XLA Ops:
  3.1 6.1 %copy-start.2 = (s32[480]{0:T(512)S(1)}, s32[480]{0:T(512)}, u32[]{:S(2)}) copy-start(s32[480]{0:T(512)} %vir_ref.3) | copy-start | bytes 5764
  3.1 6.1 %copy-start.3 = (s32[64]{0:T(128)S(1)}, s32[64]{0:T(128)}, u32[]{:S(2)}) copy-start(s32[64]{0:T(128)} %owner_ref.3) | copy-start | bytes 772
  3.2 6.1 %copy-start.4 = (s32[40]{0:T(128)S(1)}, s32[40]{0:T(128)}, u32[]{:S(2)}) copy-start(s32[40]{0:T(128)} %occ_ref.1) | copy-start | bytes 484
  3.2 29.8 %all-to-all-start = ((f32[8,32,1920]{2,1,0:T(8,128)}), f32[8,32,1920]{2,1,0:T(8,128)S(1)}, u32[]{:S(2)}, u32[]{:S(2)}) async-start(f32[8,32,1920]{2,1,0:T(8,128)} %pack.1), calls=%async_computation | async-start | bytes 3932160 | tf_op jit(solution)/shard_map/all_to_all | solution.py:431
  9.3 1.8 %copy-start = (f32[200,3600]{1,0:T(8,128)S(1)}, f32[200,3600]{1,0:T(8,128)}, u32[]{:S(2)}) copy-start(f32[200,3600]{1,0:T(8,128)} %amp_ref.1) | copy-start | bytes 8640004
  11.1 0.9 %copy-start.1 = (f32[40,480]{1,0:T(8,128)S(1)}, f32[40,480]{1,0:T(8,128)}, u32[]{:S(2)}) copy-start(f32[40,480]{1,0:T(8,128)} %singles_ref.1) | copy-start | bytes 230404
  35.4 4.6 %collective-permute-start = (f32[32,4,128]{2,1,0:T(4,128)S(1)}, f32[32,4,128]{2,1,0:T(4,128)S(1)}, u32[]{:S(2)}, u32[]{:S(2)}) collective-permute-start(f32[32,4,128]{2,1,0:T(4,128)S(1)} %get-tuple-element.13), channel_id=1, source_target_pairs={{0,1},{1,0},{2,3},{3,2},{4,5},{5,4},{6,7},{7,6},{8,9},{9,8},{10,11... | collective-permute-start | bytes 196616 | tf_op jit(solution)/shard_map/ppermute | solution.py:436
